TPU v7x, 128 devices: a whole 4x4x4 slice. The times are simulated.
128 devices in a mesh: pipe: 8 (over x, y_hi), expert: 16 (over y_lo, z, core).
Axes of the slice: x: 4, y: 4 (y_hi: 2, y_lo: 2; y = y_hi * 2 + y_lo), z: 4, core: 2. Of those that a mesh axis runs over, the one named last changes fastest.
Arguments:
- acts: bfloat16 [8, 2048, 3584], P('pipe', 'expert'), may hold values from -6 to 6
- grad_out: bfloat16 [8, 2048, 3584], P('pipe', 'expert'), may hold values from -6 to 6
- expert_ids: int32 [8, 2048, 2], P('pipe', 'expert'), may hold values from 0 to 7, all different within a row; in each aligned block of 64 rows (0 to 63, 64 to 127, ..., all dimensions but the last counted through in order) at most 24 rows name the same one
- route_weights: float32 [8, 2048, 2], P('pipe', 'expert'), may hold values from 0.1 to 1
- w_gate: bfloat16 [8, 3584, 8192], P('pipe', None, 'expert'), may hold values from -0.09375 to 0.09375
- w_up: bfloat16 [8, 3584, 8192], P('pipe', None, 'expert'), may hold values from -0.09375 to 0.09375
- w_down: bfloat16 [8, 8192, 3584], P('pipe', 'expert'), may hold values from -0.1875 to 0.1875
Outputs:
- out_acts: bfloat16 [8, 2048, 3584], P('pipe', 'expert')
- grad_acts: bfloat16 [8, 2048, 3584], P('pipe', 'expert')
- grad_gate: bfloat16 [8, 3584, 4096], P('pipe', None, 'expert')
- grad_up: bfloat16 [8, 3584, 4096], P('pipe', None, 'expert')
- grad_down: bfloat16 [8, 4096, 3584], P('pipe', 'expert')
Inputs may be any that keep to these rules, and one draw needn't show every extreme that they name: `expert_ids`: in each aligned block of 64 rows of one rank (one micro-batch of one device), no expert is named by more than 24 rows; the 2 experts of a row differ.
All inputs are finite; a program needn't handle non-finite values.
Results may differ from a plain program's by a relative error of at most 0.0072.
Values may be sent and summed in bfloat16 or wider, within the bound.
A program may use at most 192 MiB of HBM per device.

v0:
```python
import jax
import jax.numpy as jnp
from jax import lax
from jax.sharding import PartitionSpec as P

TOPK = 2
MB = 2
TOK_MB = 64


def expert_half(rows_in, rows_grad, gate_weight, up_weight, down_weight):
    pre_gate = jnp.dot(rows_in, gate_weight, preferred_element_type=jnp.float32)
    pre_up = jnp.dot(rows_in, up_weight, preferred_element_type=jnp.float32)
    sigma = jax.nn.sigmoid(pre_gate)
    active = pre_gate * sigma
    hidden = (active * pre_up).astype(jnp.bfloat16)
    part_out = jnp.dot(hidden, down_weight, preferred_element_type=jnp.float32).astype(jnp.bfloat16)
    hidden_grad = lax.dot_general(
        rows_grad, down_weight, (((1,), (1,)), ((), ())), preferred_element_type=jnp.float32
    )
    gate_grad = (hidden_grad * pre_up * sigma * (1.0 + pre_gate * (1.0 - sigma))).astype(
        jnp.bfloat16
    )
    up_grad = (hidden_grad * active).astype(jnp.bfloat16)
    part_input = lax.dot_general(
        gate_grad, gate_weight, (((1,), (1,)), ((), ())), preferred_element_type=jnp.float32
    )
    part_input = part_input + lax.dot_general(
        up_grad, up_weight, (((1,), (1,)), ((), ())), preferred_element_type=jnp.float32
    )
    grad_gate = lax.dot_general(
        rows_in, gate_grad, (((0,), (0,)), ((), ())), preferred_element_type=jnp.float32
    )
    grad_up = lax.dot_general(
        rows_in, up_grad, (((0,), (0,)), ((), ())), preferred_element_type=jnp.float32
    )
    grad_down = lax.dot_general(
        hidden, rows_grad, (((0,), (0,)), ((), ())), preferred_element_type=jnp.float32
    )
    return (part_out, part_input.astype(jnp.bfloat16), grad_gate, grad_up, grad_down)


def flip_blocks(array, block_count):
    shaped = array.reshape((block_count, array.shape[0] // block_count) + array.shape[1:])
    return jnp.flip(shaped, axis=0).reshape(array.shape)


def on_device(acts, grad_out, expert_ids, route_weights, w_gate, w_up, w_down):
    token_rows = acts[0]
    grad_rows = grad_out[0]
    choice_ids = expert_ids[0]
    choice_gain = route_weights[0]
    gate_weight = w_gate[0]
    up_weight = w_up[0]
    down_weight = w_down[0]
    groups = lax.axis_size("expert")
    expert_count = groups // 2
    capacity = 3 * TOPK * TOK_MB // (2 * expert_count)
    slot_count = expert_count * capacity
    model_width = gate_weight.shape[0]
    unit_count = gate_weight.shape[1]
    rows_dims = (((0,), (0,)), ((), ()))
    slot_dims = (((1,), (0,)), ((), ()))
    slot_range = jnp.arange(slot_count, dtype=jnp.int32)
    expert_range = jnp.arange(expert_count, dtype=jnp.int32)
    acc_gate = jnp.zeros((model_width, unit_count), jnp.float32)
    acc_up = jnp.zeros((model_width, unit_count), jnp.float32)
    acc_down = jnp.zeros((unit_count, model_width), jnp.float32)
    out_pieces = []
    input_pieces = []
    for batch_index in range(MB):
        first_row = batch_index * TOK_MB
        batch_tokens = token_rows[first_row : first_row + TOK_MB]
        batch_grads = grad_rows[first_row : first_row + TOK_MB]
        batch_ids = choice_ids[first_row : first_row + TOK_MB]
        batch_gain = choice_gain[first_row : first_row + TOK_MB]
        flat_ids = batch_ids.reshape(-1)
        member = (flat_ids[:, None] == expert_range[None, :]).astype(jnp.int32)
        running = jnp.cumsum(member, axis=0) - 1
        slot_rank = jnp.sum(member * running, axis=1)
        target = (flat_ids * capacity + slot_rank).reshape(TOK_MB, TOPK)
        matches = (target[:, :, None] == slot_range[None, None, :]).astype(jnp.float32)
        placing = jnp.sum(matches, axis=1)
        weighting = jnp.sum(matches * batch_gain[:, :, None], axis=1)
        slot_tokens = lax.dot_general(
            placing.astype(jnp.bfloat16),
            batch_tokens,
            rows_dims,
            preferred_element_type=jnp.float32,
        ).astype(jnp.bfloat16)
        slot_grads = lax.dot_general(
            weighting,
            batch_grads.astype(jnp.float32),
            rows_dims,
            precision=lax.Precision.HIGHEST,
            preferred_element_type=jnp.float32,
        ).astype(jnp.bfloat16)
        send_tokens = jnp.repeat(
            slot_tokens.reshape(expert_count, capacity, model_width), 2, axis=0
        )
        send_grads = jnp.repeat(slot_grads.reshape(expert_count, capacity, model_width), 2, axis=0)
        recv_tokens, recv_grads = (
            lax.all_to_all(send_tokens, "expert", split_axis=0, concat_axis=0, tiled=True),
            lax.all_to_all(send_grads, "expert", split_axis=0, concat_axis=0, tiled=True),
        )
        part_out, part_input, grad_g, grad_u, grad_d = expert_half(
            recv_tokens.reshape(groups * capacity, model_width),
            recv_grads.reshape(groups * capacity, model_width),
            gate_weight,
            up_weight,
            down_weight,
        )
        back_out, back_input = (
            lax.all_to_all(
                part_out.reshape(groups, capacity, model_width),
                "expert",
                split_axis=0,
                concat_axis=0,
                tiled=True,
            ),
            lax.all_to_all(
                part_input.reshape(groups, capacity, model_width),
                "expert",
                split_axis=0,
                concat_axis=0,
                tiled=True,
            ),
        )
        slot_out = (
            jnp.sum(
                back_out.reshape(expert_count, 2, capacity, model_width).astype(jnp.float32), axis=1
            )
            .astype(jnp.bfloat16)
            .reshape(slot_count, model_width)
        )
        slot_input = (
            jnp.sum(
                back_input.reshape(expert_count, 2, capacity, model_width).astype(jnp.float32),
                axis=1,
            )
            .astype(jnp.bfloat16)
            .reshape(slot_count, model_width)
        )
        acc_gate = acc_gate + grad_g
        acc_up = acc_up + grad_u
        acc_down = acc_down + grad_d
        batch_out = lax.dot_general(
            weighting,
            slot_out.astype(jnp.float32),
            slot_dims,
            precision=lax.Precision.HIGHEST,
            preferred_element_type=jnp.float32,
        )
        batch_input = lax.dot_general(
            placing,
            slot_input.astype(jnp.float32),
            slot_dims,
            precision=lax.Precision.HIGHEST,
            preferred_element_type=jnp.float32,
        )
        out_pieces.append(batch_out.astype(jnp.bfloat16))
        input_pieces.append(batch_input.astype(jnp.bfloat16))
    local_gate = acc_gate.astype(jnp.bfloat16)
    local_up = acc_up.astype(jnp.bfloat16)
    local_down = acc_down.astype(jnp.bfloat16)
    rank_index = lax.axis_index("pipe")
    rank_count = lax.axis_size("pipe")
    kept_half = (rank_index >= rank_count // 2).astype(jnp.int32)
    half_units = unit_count // 2
    own_gate = lax.dynamic_slice_in_dim(local_gate, kept_half * half_units, half_units, 1)
    own_up = lax.dynamic_slice_in_dim(local_up, kept_half * half_units, half_units, 1)
    own_down = lax.dynamic_slice_in_dim(local_down, kept_half * half_units, half_units, 0)
    carried = (
        lax.dynamic_slice_in_dim(local_gate, (1 - kept_half) * half_units, half_units, 1),
        lax.dynamic_slice_in_dim(local_up, (1 - kept_half) * half_units, half_units, 1),
        lax.dynamic_slice_in_dim(local_down, (1 - kept_half) * half_units, half_units, 0),
    )
    spread = (
        lax.all_to_all(carried[0], "pipe", split_axis=0, concat_axis=0, tiled=True),
        lax.all_to_all(carried[1], "pipe", split_axis=0, concat_axis=0, tiled=True),
        lax.all_to_all(carried[2], "pipe", split_axis=0, concat_axis=0, tiled=True),
    )
    flipped = (
        flip_blocks(spread[0], rank_count),
        flip_blocks(spread[1], rank_count),
        flip_blocks(spread[2], rank_count),
    )
    carried = (
        lax.all_to_all(flipped[0], "pipe", split_axis=0, concat_axis=0, tiled=True),
        lax.all_to_all(flipped[1], "pipe", split_axis=0, concat_axis=0, tiled=True),
        lax.all_to_all(flipped[2], "pipe", split_axis=0, concat_axis=0, tiled=True),
    )
    grad_gate = (own_gate.astype(jnp.float32) + carried[0].astype(jnp.float32)).astype(jnp.bfloat16)
    grad_up = (own_up.astype(jnp.float32) + carried[1].astype(jnp.float32)).astype(jnp.bfloat16)
    grad_down = (own_down.astype(jnp.float32) + carried[2].astype(jnp.float32)).astype(jnp.bfloat16)
    out_acts = jnp.concatenate(out_pieces, axis=0)[None]
    grad_acts = jnp.concatenate(input_pieces, axis=0)[None]
    return (out_acts, grad_acts, grad_gate[None], grad_up[None], grad_down[None])


def solution(mesh):
    placed = (
        P("pipe", "expert", None),
        P("pipe", "expert", None),
        P("pipe", "expert", None),
        P("pipe", "expert", None),
        P("pipe", None, "expert"),
        P("pipe", None, "expert"),
        P("pipe", "expert", None),
    )
    return jax.shard_map(
        on_device,
        mesh=mesh,
        in_specs=placed,
        out_specs=(
            P("pipe", "expert", None),
            P("pipe", "expert", None),
            P("pipe", None, "expert"),
            P("pipe", None, "expert"),
            P("pipe", "expert", None),
        ),
        check_vma=False,
    )
```

profile of v0, /device:TPU:96, one launch (start us, length us, event | category | flops | bytes accessed | tf_op | source)
XLA Modules:
  0.0 585.9 jit_solution(2772636694157641651)
XLA Ops:
  7.3 1.7 broadcast_in_dim.33
  9.0 5.5 all-to-all-start
  14.5 3.4 convolution_convert_fusion.3
  17.9 36.2 %all-to-all-done = bf16[16,24,3584]{2,1,0:T(8,128)(2,1)S(1)} async-done(((bf16[16,24,3584]{2,1,0:T(8,128)(2,1)}), bf16[16,24,3584]{2,1,0:T(8,128)(2,1)S(1)}, u32[]{:S(2)}, u32[]{:S(2)}) %all-to-all-start) | async-done | bytes 2752544 | tf_op jit(solution)/shard_map/all_to_all | solution.py:103
  54.1 4.1 broadcast_in_dim.36
  58.2 4.9 all-to-all-start.4
  64.7 38.1 %all-to-all-done.4 = bf16[16,24,3584]{2,1,0:T(8,128)(2,1)} async-done(((bf16[16,24,3584]{2,1,0:T(8,128)(2,1)}), bf16[16,24,3584]{2,1,0:T(8,128)(2,1)}, u32[]{:S(2)}, u32[]{:S(2)}) %all-to-all-start.4) | async-done | bytes 2752544 | tf_op jit(solution)/shard_map/all_to_all | solution.py:104
  102.7 1.7 broadcast_in_dim.34
  104.5 4.9 all-to-all-start.2
  109.4 3.4 convolution_convert_fusion.2
  112.8 5.3 fusion.15
  118.1 30.8 %all-to-all-done.2 = bf16[16,24,3584]{2,1,0:T(8,128)(2,1)S(1)} async-done(((bf16[16,24,3584]{2,1,0:T(8,128)(2,1)}), bf16[16,24,3584]{2,1,0:T(8,128)(2,1)S(1)}, u32[]{:S(2)}, u32[]{:S(2)}) %all-to-all-start.2) | async-done | bytes 2752544 | tf_op jit(solution)/shard_map/all_to_all | solution.py:103
  149.0 3.1 broadcast_in_dim.37
  152.0 5.5 all-to-all-start.6
  157.6 4.6 fusion.23
  162.2 3.6 multiply_convert_fusion.2
  165.9 7.0 %fusion.45 = f32[512,3584]{1,0:T(8,128)} fusion(bf16[384,512]{1,0:T(8,128)(2,1)S(1)} %get-tuple-element.11, bf16[384,3584]{1,0:T(8,128)(2,1)} %bitcast.25), kind=kOutput, calls=%fused_computation.94 | convolution fusion | flops 1409286144 | bytes 10485760 | tf_op jit(solution)/shard_map/dot_general | solution.py:37
  172.9 2.5 fusion.13
  175.4 2.5 fusion.21
  177.9 19.2 %all-to-all-done.6 = bf16[16,24,3584]{2,1,0:T(8,128)(2,1)} async-done(((bf16[16,24,3584]{2,1,0:T(8,128)(2,1)}), bf16[16,24,3584]{2,1,0:T(8,128)(2,1)}, u32[]{:S(2)}, u32[]{:S(2)}) %all-to-all-start.6) | async-done | bytes 2752544 | tf_op jit(solution)/shard_map/all_to_all | solution.py:104
  197.1 6.0 %multiply_convert_fusion = (bf16[384,512]{1,0:T(8,128)(2,1)}, bf16[384,512]{1,0:T(8,128)(2,1)}, bf16[384,512]{1,0:T(8,128)(2,1)S(1)}) fusion(f32[384,512]{1,0:T(8,128)} %fusion.21, f32[384,512]{1,0:T(8,128)} %fusion.13, bf16[384,3584]{1,0:T(8,128)(2,1)} %bitcast.32, bf16[1,512,3584]{2,1,0:T(8,128)(2,1)} %param.13), kind=kOutput, calls=%fused_computation.52 | convolution fusion | flops 1412235264 | bytes 9175040 | tf_op jit(solution)/shard_map/dot_general | solution.py:18
  203.1 6.1 %add_convert_fusion = bf16[512,3584]{1,0:T(8,128)(2,1)S(1)} fusion(f32[512,3584]{1,0:T(8,128)} %fusion.45, bf16[384,512]{1,0:T(8,128)(2,1)S(1)} %get-tuple-element.14, bf16[384,3584]{1,0:T(8,128)(2,1)} %bitcast.32), kind=kOutput, calls=%fused_computation | convolution fusion | flops 1412956160 | bytes 14155776 | tf_op jit(solution)/shard_map/dot_general | solution.py:37
  209.3 1.8 copy-done.4
  212.5 6.9 %all-to-all-start.12 = ((bf16[8,32,3584]{2,1,0:T(8,128)(2,1)}), bf16[8,32,3584]{2,1,0:T(8,128)(2,1)}, u32[]{:S(2)}, u32[]{:S(2)}) async-start(bf16[8,32,3584]{2,1,0:T(8,128)(2,1)} %bitcast.151), calls=%async_computation.12 | async-start | bytes 3670016 | tf_op jit(solution)/shard_map/all_to_all | solution.py:181
  219.3 3.9 fusion.44
  223.3 2.2 add_convert_fusion.1
  225.5 1.8 copy-done
  228.6 18.9 %all-to-all-done.12 = bf16[8,32,3584]{2,1,0:T(8,128)(2,1)} async-done(((bf16[8,32,3584]{2,1,0:T(8,128)(2,1)}), bf16[8,32,3584]{2,1,0:T(8,128)(2,1)}, u32[]{:S(2)}, u32[]{:S(2)}) %all-to-all-start.12) | async-done | bytes 1835040 | tf_op jit(solution)/shard_map/all_to_all | solution.py:181
  247.6 4.3 all-to-all-start.10
  251.9 3.9 fusion.43
  255.9 2.2 add_convert_fusion.2
  258.1 1.9 copy-done.2
  261.3 17.3 %all-to-all-done.10 = bf16[8,448,256]{2,1,0:T(8,128)(2,1)} async-done(((bf16[8,448,256]{2,1,0:T(8,128)(2,1)}), bf16[8,448,256]{2,1,0:T(8,128)(2,1)}, u32[]{:S(2)}, u32[]{:S(2)}) %all-to-all-start.10) | async-done | bytes 1835040 | tf_op jit(solution)/shard_map/all_to_all | solution.py:180
  278.7 3.6 all-to-all-start.8
  282.3 3.8 fusion.19
  286.1 3.3 fusion
  289.4 18.9 %all-to-all-done.8 = bf16[8,448,256]{2,1,0:T(8,128)(2,1)S(1)} async-done(((bf16[8,448,256]{2,1,0:T(8,128)(2,1)}), bf16[8,448,256]{2,1,0:T(8,128)(2,1)S(1)}, u32[]{:S(2)}, u32[]{:S(2)}) %all-to-all-start.8) | async-done | bytes 1835040 | tf_op jit(solution)/shard_map/all_to_all | solution.py:179
  309.4 4.8 all-to-all-start.5
  314.3 3.8 fusion.17
  318.1 3.1 fusion.1
  321.3 32.5 %all-to-all-done.5 = bf16[16,24,3584]{2,1,0:T(8,128)(2,1)S(1)} async-done(((bf16[16,24,3584]{2,1,0:T(8,128)(2,1)}), bf16[16,24,3584]{2,1,0:T(8,128)(2,1)S(1)}, u32[]{:S(2)}, u32[]{:S(2)}) %all-to-all-start.5) | async-done | bytes 2752544 | tf_op jit(solution)/shard_map/all_to_all | solution.py:121
  353.7 5.1 all-to-all-start.7
  358.8 5.2 convolution_convert_fusion.1
  364.0 34.5 %all-to-all-done.7 = bf16[16,24,3584]{2,1,0:T(8,128)(2,1)} async-done(((bf16[16,24,3584]{2,1,0:T(8,128)(2,1)}), bf16[16,24,3584]{2,1,0:T(8,128)(2,1)}, u32[]{:S(2)}, u32[]{:S(2)}) %all-to-all-start.7) | async-done | bytes 2752544 | tf_op jit(solution)/shard_map/all_to_all | solution.py:121
  398.4 5.1 all-to-all-start.1
  403.5 5.2 convolution_convert_fusion
  408.7 34.4 %all-to-all-done.1 = bf16[16,24,3584]{2,1,0:T(8,128)(2,1)} async-done(((bf16[16,24,3584]{2,1,0:T(8,128)(2,1)}), bf16[16,24,3584]{2,1,0:T(8,128)(2,1)}, u32[]{:S(2)}, u32[]{:S(2)}) %all-to-all-start.1) | async-done | bytes 2752544 | tf_op jit(solution)/shard_map/all_to_all | solution.py:114
  443.2 4.9 all-to-all-start.3
  448.1 2.9 all_to_all.78
  451.0 36.8 %all-to-all-done.3 = bf16[16,24,3584]{2,1,0:T(8,128)(2,1)} async-done(((bf16[16,24,3584]{2,1,0:T(8,128)(2,1)}), bf16[16,24,3584]{2,1,0:T(8,128)(2,1)}, u32[]{:S(2)}, u32[]{:S(2)}) %all-to-all-start.3) | async-done | bytes 2752544 | tf_op jit(solution)/shard_map/all_to_all | solution.py:114
  487.7 4.3 all-to-all-start.13
  492.1 2.8 all_to_all.74
  494.9 2.8 all_to_all.70
  498.3 2.3 bitcast_reduce_fusion
  500.6 2.3 bitcast_reduce_fusion.3
  506.1 14.6 %all-to-all-done.13 = bf16[8,32,3584]{2,1,0:T(8,128)(2,1)} async-done(((bf16[8,32,3584]{2,1,0:T(8,128)(2,1)}), bf16[8,32,3584]{2,1,0:T(8,128)(2,1)}, u32[]{:S(2)}, u32[]{:S(2)}) %all-to-all-start.13) | async-done | bytes 1835040 | tf_op jit(solution)/shard_map/all_to_all | solution.py:191
  520.8 4.0 all-to-all-start.11
  524.8 2.3 bitcast_reduce_fusion.2
  530.8 20.8 %all-to-all-done.11 = bf16[8,448,256]{2,1,0:T(8,128)(2,1)S(1)} async-done(((bf16[8,448,256]{2,1,0:T(8,128)(2,1)}), bf16[8,448,256]{2,1,0:T(8,128)(2,1)S(1)}, u32[]{:S(2)}, u32[]{:S(2)}) %all-to-all-start.11) | async-done | bytes 1835040 | tf_op jit(solution)/shard_map/all_to_all | solution.py:190
  551.6 4.3 all-to-all-start.9
  555.9 3.9 fusion.27
  559.8 1.8 fusion.26
  561.6 20.4 %all-to-all-done.9 = bf16[8,448,256]{2,1,0:T(8,128)(2,1)} async-done(((bf16[8,448,256]{2,1,0:T(8,128)(2,1)}), bf16[8,448,256]{2,1,0:T(8,128)(2,1)}, u32[]{:S(2)}, u32[]{:S(2)}) %all-to-all-start.9) | async-done | bytes 1835040 | tf_op jit(solution)/shard_map/all_to_all | solution.py:189
  582.0 3.7 fusion.25
  (87 shorter events, 20.8 us)
Async XLA Ops:
  5.1 0.6 copy-start.24
  5.1 9.4 %copy-start.20 = (f32[64,192]{1,0:T(8,128)}, f32[64,192]{1,0:T(8,128)S(1)}, u32[]{:S(2)}) copy-start(f32[64,192]{1,0:T(8,128)S(1)} %get-tuple-element.21) | copy-start | bytes 147460
  5.1 58.0 %copy-start.22 = (f32[64,192]{1,0:T(8,128)}, f32[64,192]{1,0:T(8,128)S(1)}, u32[]{:S(2)}) copy-start(f32[64,192]{1,0:T(8,128)S(1)} %get-tuple-element.7) | copy-start | bytes 147460
  5.1 104.3 %copy-start.18 = (f32[64,192]{1,0:T(8,128)}, f32[64,192]{1,0:T(8,128)S(1)}, u32[]{:S(2)}) copy-start(f32[64,192]{1,0:T(8,128)S(1)} %get-tuple-element.8) | copy-start | bytes 147460
  9.0 45.1 %all-to-all-start = ((bf16[16,24,3584]{2,1,0:T(8,128)(2,1)}), bf16[16,24,3584]{2,1,0:T(8,128)(2,1)S(1)}, u32[]{:S(2)}, u32[]{:S(2)}) async-start(bf16[16,24,3584]{2,1,0:T(8,128)(2,1)} %bitcast.147), calls=%async_computation | async-start | bytes 5505024 | tf_op jit(solution)/shard_map/all_to_all | solution.py:103
  54.1 4.1 copy-start.3
  58.2 44.6 %all-to-all-start.4 = ((bf16[16,24,3584]{2,1,0:T(8,128)(2,1)}), bf16[16,24,3584]{2,1,0:T(8,128)(2,1)}, u32[]{:S(2)}, u32[]{:S(2)}) async-start(bf16[16,24,3584]{2,1,0:T(8,128)(2,1)} %bitcast.148), calls=%async_computation.4 | async-start | bytes 5505024 | tf_op jit(solution)/shard_map/all_to_all | solution.py:104
  104.5 44.5 %all-to-all-start.2 = ((bf16[16,24,3584]{2,1,0:T(8,128)(2,1)}), bf16[16,24,3584]{2,1,0:T(8,128)(2,1)S(1)}, u32[]{:S(2)}, u32[]{:S(2)}) async-start(bf16[16,24,3584]{2,1,0:T(8,128)(2,1)} %bitcast.143), calls=%async_computation.2 | async-start | bytes 5505024 | tf_op jit(solution)/shard_map/all_to_all | solution.py:103
  152.0 45.1 %all-to-all-start.6 = ((bf16[16,24,3584]{2,1,0:T(8,128)(2,1)}), bf16[16,24,3584]{2,1,0:T(8,128)(2,1)}, u32[]{:S(2)}, u32[]{:S(2)}) async-start(bf16[16,24,3584]{2,1,0:T(8,128)(2,1)} %bitcast.144), calls=%async_computation.6 | async-start | bytes 5505024 | tf_op jit(solution)/shard_map/all_to_all | solution.py:104
  157.6 4.6 copy-start.28
  157.6 4.6 copy-start.29
  165.9 7.0 %copy-start.26 = (bf16[384,512]{1,0:T(8,128)(2,1)}, bf16[384,512]{1,0:T(8,128)(2,1)S(1)}, u32[]{:S(2)}) copy-start(bf16[384,512]{1,0:T(8,128)(2,1)S(1)} %get-tuple-element.11) | copy-start | bytes 1179652
  165.9 7.0 %copy-start.6 = (bf16[1,3584,512]{2,1,0:T(8,128)(2,1)S(1)}, bf16[1,3584,512]{2,1,0:T(8,128)(2,1)}, u32[]{:S(2)}) copy-start(bf16[1,3584,512]{2,1,0:T(8,128)(2,1)} %param.12) | copy-start | bytes 11010052
  172.9 2.5 copy-start.5
  203.1 6.2 %copy-start.16 = (bf16[384,512]{1,0:T(8,128)(2,1)}, bf16[384,512]{1,0:T(8,128)(2,1)S(1)}, u32[]{:S(2)}) copy-start(bf16[384,512]{1,0:T(8,128)(2,1)S(1)} %get-tuple-element.14) | copy-start | bytes 1179652
  209.3 1.8 copy-start.4
  212.5 35.1 %all-to-all-start.12 = ((bf16[8,32,3584]{2,1,0:T(8,128)(2,1)}), bf16[8,32,3584]{2,1,0:T(8,128)(2,1)}, u32[]{:S(2)}, u32[]{:S(2)}) async-start(bf16[8,32,3584]{2,1,0:T(8,128)(2,1)} %bitcast.151), calls=%async_computation.12 | async-start | bytes 3670016 | tf_op jit(solution)/shard_map/all_to_all | solution.py:181
  219.3 3.9 copy-start.12
  225.5 1.8 copy-start
  247.6 31.1 %all-to-all-start.10 = ((bf16[8,448,256]{2,1,0:T(8,128)(2,1)}), bf16[8,448,256]{2,1,0:T(8,128)(2,1)}, u32[]{:S(2)}, u32[]{:S(2)}) async-start(bf16[8,448,256]{2,1,0:T(8,128)(2,1)} %bitcast.149), calls=%async_computation.10 | async-start | bytes 3670016 | tf_op jit(solution)/shard_map/all_to_all | solution.py:180
  251.9 3.9 copy-start.14
  258.1 1.9 copy-start.2
  278.7 29.6 %all-to-all-start.8 = ((bf16[8,448,256]{2,1,0:T(8,128)(2,1)}), bf16[8,448,256]{2,1,0:T(8,128)(2,1)S(1)}, u32[]{:S(2)}, u32[]{:S(2)}) async-start(bf16[8,448,256]{2,1,0:T(8,128)(2,1)} %bitcast.150), calls=%async_computation.8 | async-start | bytes 3670016 | tf_op jit(solution)/shard_map/all_to_all | solution.py:179
  282.3 3.8 copy-start.7
  308.2 1.2 copy-start.9
  308.2 6.1 %copy-start.15 = (bf16[384,512]{1,0:T(8,128)(2,1)S(1)}, bf16[384,512]{1,0:T(8,128)(2,1)}, u32[]{:S(2)}) copy-start(bf16[384,512]{1,0:T(8,128)(2,1)} %get-tuple-element.13) | copy-start | bytes 1179652
  309.4 44.3 %all-to-all-start.5 = ((bf16[16,24,3584]{2,1,0:T(8,128)(2,1)}), bf16[16,24,3584]{2,1,0:T(8,128)(2,1)S(1)}, u32[]{:S(2)}, u32[]{:S(2)}) async-start(bf16[16,24,3584]{2,1,0:T(8,128)(2,1)} %bitcast.145), calls=%async_computation.5 | async-start | bytes 5505024 | tf_op jit(solution)/shard_map/all_to_all | solution.py:121
  314.3 3.8 copy-start.8
  314.3 3.8 copy-start.13
  353.7 5.1 copy-start.27
  353.7 44.7 %all-to-all-start.7 = ((bf16[16,24,3584]{2,1,0:T(8,128)(2,1)}), bf16[16,24,3584]{2,1,0:T(8,128)(2,1)}, u32[]{:S(2)}, u32[]{:S(2)}) async-start(bf16[16,24,3584]{2,1,0:T(8,128)(2,1)} %bitcast.146), calls=%async_computation.7 | async-start | bytes 5505024 | tf_op jit(solution)/shard_map/all_to_all | solution.py:121
  398.4 5.1 copy-start.17
  398.4 44.7 %all-to-all-start.1 = ((bf16[16,24,3584]{2,1,0:T(8,128)(2,1)}), bf16[16,24,3584]{2,1,0:T(8,128)(2,1)}, u32[]{:S(2)}, u32[]{:S(2)}) async-start(bf16[16,24,3584]{2,1,0:T(8,128)(2,1)} %bitcast.160), calls=%async_computation.1 | async-start | bytes 5505024 | tf_op jit(solution)/shard_map/all_to_all | solution.py:114
  443.2 44.6 %all-to-all-start.3 = ((bf16[16,24,3584]{2,1,0:T(8,128)(2,1)}), bf16[16,24,3584]{2,1,0:T(8,128)(2,1)}, u32[]{:S(2)}, u32[]{:S(2)}) async-start(bf16[16,24,3584]{2,1,0:T(8,128)(2,1)} %bitcast.161), calls=%async_computation.3 | async-start | bytes 5505024 | tf_op jit(solution)/shard_map/all_to_all | solution.py:114
  487.7 33.0 %all-to-all-start.13 = ((bf16[8,32,3584]{2,1,0:T(8,128)(2,1)}), bf16[8,32,3584]{2,1,0:T(8,128)(2,1)}, u32[]{:S(2)}, u32[]{:S(2)}) async-start(bf16[8,32,3584]{2,1,0:T(8,128)(2,1)} %all_to_all.78), calls=%async_computation.13 | async-start | bytes 3670016 | tf_op jit(solution)/shard_map/all_to_all | solution.py:191
  500.6 2.3 copy-start.25
  500.6 3.9 copy-start.23
  520.8 30.8 %all-to-all-start.11 = ((bf16[8,448,256]{2,1,0:T(8,128)(2,1)}), bf16[8,448,256]{2,1,0:T(8,128)(2,1)S(1)}, u32[]{:S(2)}, u32[]{:S(2)}) async-start(bf16[8,448,256]{2,1,0:T(8,128)(2,1)} %all_to_all.74), calls=%async_computation.11 | async-start | bytes 3670016 | tf_op jit(solution)/shard_map/all_to_all | solution.py:190
  524.8 2.4 copy-start.21
  524.8 3.2 copy-start.19
  527.1 1.7 copy-start.10
  527.1 1.7 copy-start.11
  551.6 30.4 %all-to-all-start.9 = ((bf16[8,448,256]{2,1,0:T(8,128)(2,1)}), bf16[8,448,256]{2,1,0:T(8,128)(2,1)}, u32[]{:S(2)}, u32[]{:S(2)}) async-start(bf16[8,448,256]{2,1,0:T(8,128)(2,1)} %all_to_all.70), calls=%async_computation.9 | async-start | bytes 3670016 | tf_op jit(solution)/shard_map/all_to_all | solution.py:189
  555.9 3.9 copy-start.1
where the time goes:
time: 592 us; the launch traced here: 586 us
  waiting for transfers between devices  373 us (63%)
  matrix products  89 us (15%)
  starting transfers between devices  68.3 us (12%)
  local copies, waits for them, and re-layouts  33.2 us (6%)
  other arithmetic  20.6 us (3%)
    all_to_all x2, waiting for transfers between devices, on_device(): lax.all_to_all(part_out.reshape(groups, capacity, model_width), 'expert',...  71.2 us
    all_to_all x2, waiting for transfers between devices, on_device(): lax.all_to_all(send_tokens, 'expert', split_axis=0, concat_axis=0, tiled=...  67 us
    all_to_all x2, waiting for transfers between devices, on_device(): lax.all_to_all(part_input.reshape(groups, capacity, model_width), 'expert...  66.9 us
    all_to_all x2, waiting for transfers between devices, on_device(): lax.all_to_all(send_grads, 'expert', split_axis=0, concat_axis=0, tiled=T...  57.3 us
    all_to_all x1, waiting for transfers between devices, on_device(): lax.all_to_all(flipped[1], 'pipe', split_axis=0, concat_axis=0, tiled=True)  20.8 us
    all_to_all x1, waiting for transfers between devices, on_device(): lax.all_to_all(flipped[0], 'pipe', split_axis=0, concat_axis=0, tiled=True)  20.4 us
    all_to_all x1, waiting for transfers between devices, on_device(): lax.all_to_all(carried[2], 'pipe', split_axis=0, concat_axis=0, tiled=True)  18.9 us
    all_to_all x1, waiting for transfers between devices, on_device(): lax.all_to_all(carried[0], 'pipe', split_axis=0, concat_axis=0, tiled=True)  18.9 us
  transfers between devices with their start and end apart: 14, of which 14 were waited for; matrix products, arithmetic and copies ran while one was open for 16% of the time, Pallas kernels for 0%

commit v1 on v0

v1 whole, which is shorter than its diff:
```python
import functools

import jax
import jax.numpy as jnp
from jax import lax
from jax.experimental import pallas as pl
from jax.experimental.pallas import tpu as pltpu
from jax.sharding import PartitionSpec as P

MESH = pl.DeviceIdType.MESH
CHIPS = 8
CAP = 48


def place():
    pipe = lax.axis_index("pipe")
    own = lax.axis_index("expert")
    return pipe, own, own // 8, (own // 2) % 4, own % 2


def chip_at(y, z, k, sign):
    return ((y + k // 4) % 2) * 4 + (z + 4 + sign * (k % 4)) % 4


def greet(pipe, own, y, z, core):
    barrier = pltpu.get_barrier_semaphore()
    for k in range(1, CHIPS):
        peer = chip_at(y, z, k, 1) * 2 + core
        pl.semaphore_signal(barrier, inc=1, device_id=(pipe, peer), device_id_type=MESH)
    sibling = own + 1 - 2 * core
    pl.semaphore_signal(barrier, inc=1, device_id=(pipe, sibling), device_id_type=MESH)
    pl.semaphore_wait(barrier, CHIPS)
    return sibling


def dispatch_kernel(
    tokens, grads, got_tokens, got_grads, send_sem, recv_sem, near_send, near_recv, own_sem
):
    pipe, own, y, z, core = place()
    chip = own // 2
    sibling = greet(pipe, own, y, z, core)
    arrays = ((tokens, got_tokens), (grads, got_grads))

    def far(a, k):
        source, target = arrays[a]
        dest = chip_at(y, z, k, 1)
        return pltpu.make_async_remote_copy(
            src_ref=source.at[dest],
            dst_ref=target.at[own],
            send_sem=send_sem.at[a, k],
            recv_sem=recv_sem.at[a, k],
            device_id=(pipe, dest * 2 + core),
            device_id_type=MESH,
        )

    def near(a, k):
        source, target = arrays[a]
        origin = chip_at(y, z, k, -1) * 2 + core
        return pltpu.make_async_remote_copy(
            src_ref=source.at[chip] if k == 0 else target.at[origin],
            dst_ref=target.at[origin],
            send_sem=near_send.at[a, k],
            recv_sem=near_recv.at[a, k],
            device_id=(pipe, sibling),
            device_id_type=MESH,
        )

    def stay(a):
        source, target = arrays[a]
        return pltpu.make_async_copy(source.at[chip], target.at[own], own_sem.at[a])

    for a in range(2):
        for k in (6, 2, 5, 7, 1, 3, 4):
            far(a, k).start()
        stay(a).start()
        near(a, 0).start()
    for a in range(2):
        for k in (4, 1, 3, 5, 7, 2, 6):
            far(a, k).wait_recv()
            near(a, k).start()
    for a in range(2):
        stay(a).wait()
        for k in range(CHIPS):
            near(a, k).wait()
            if k:
                far(a, k).wait_send()


def dispatch(tokens, grads):
    width = tokens.shape[-1]
    anywhere = pl.BlockSpec(memory_space=pl.ANY)
    dma = pltpu.SemaphoreType.DMA
    shape = jax.ShapeDtypeStruct((2 * CHIPS, CAP, width), tokens.dtype)
    return pl.pallas_call(
        dispatch_kernel,
        name="dispatch",
        out_shape=(shape, shape),
        in_specs=[anywhere] * 2,
        out_specs=(anywhere, anywhere),
        scratch_shapes=[dma((2, CHIPS))] * 4 + [dma((2,))],
        compiler_params=pltpu.CompilerParams(collective_id=1, has_side_effects=True),
    )(tokens, grads)


def return_kernel(
    out_part,
    input_part,
    back_out,
    back_input,
    halves,
    sums,
    mine,
    send_sem,
    recv_sem,
    near_send,
    near_recv,
    mine_sem,
    own_sem,
):
    pipe, own, y, z, core = place()
    chip = own // 2
    sibling = greet(pipe, own, y, z, core)
    arrays = ((out_part, back_out), (input_part, back_input))

    def near(a, k):
        there = chip_at(y, z, k, 1) * 2 + 1 - core
        return pltpu.make_async_remote_copy(
            src_ref=arrays[a][0].at[there],
            dst_ref=halves.at[a, k],
            send_sem=near_send.at[a, k],
            recv_sem=near_recv.at[a, k],
            device_id=(pipe, sibling),
            device_id_type=MESH,
        )

    def load(a, k):
        here = chip_at(y, z, k, 1) * 2 + core
        return pltpu.make_async_copy(arrays[a][0].at[here], mine.at[a, k], mine_sem.at[a, k])

    def far(a, k):
        return pltpu.make_async_remote_copy(
            src_ref=sums.at[a, k],
            dst_ref=arrays[a][1].at[chip],
            send_sem=send_sem.at[a, k],
            recv_sem=recv_sem.at[a, k],
            device_id=(pipe, chip_at(y, z, k, 1) * 2 + core),
            device_id_type=MESH,
        )

    def stay(a):
        return pltpu.make_async_copy(sums.at[a, 0], arrays[a][1].at[chip], own_sem.at[a])

    order = (6, 2, 5, 7, 1, 3, 4, 0)
    for a in range(2):
        for k in order:
            near(a, k).start()
            load(a, k).start()
    for a in range(2):
        for k in order:
            load(a, k).wait()
            near(a, k).wait_recv()
            total = halves[a, k].astype(jnp.float32) + mine[a, k].astype(jnp.float32)
            sums[a, k] = total.astype(jnp.bfloat16)
            if k:
                far(a, k).start()
            else:
                stay(a).start()
    for a in range(2):
        stay(a).wait()
        for k in range(CHIPS):
            near(a, k).wait_send()
            if k:
                far(a, k).wait()


def give_back(out_part, input_part):
    width = out_part.shape[-1]
    anywhere = pl.BlockSpec(memory_space=pl.ANY)
    dma = pltpu.SemaphoreType.DMA
    shape = jax.ShapeDtypeStruct((CHIPS, CAP, width), out_part.dtype)
    block = pltpu.VMEM((2, CHIPS, CAP, width), out_part.dtype)
    return pl.pallas_call(
        return_kernel,
        name="give_back",
        out_shape=(shape, shape),
        in_specs=[anywhere] * 2,
        out_specs=(anywhere, anywhere),
        scratch_shapes=[block] * 3 + [dma((2, CHIPS))] * 5 + [dma((2,))],
        compiler_params=pltpu.CompilerParams(
            collective_id=2, has_side_effects=True, vmem_limit_bytes=40 << 20
        ),
    )(out_part, input_part)


def split_gain(gain):
    high = gain.astype(jnp.bfloat16)
    return high, (gain - high.astype(jnp.float32)).astype(jnp.bfloat16)


def dot(a, b, contract):
    return lax.dot_general(a, b, ((contract[:1], contract[1:]), ((), ())), preferred_element_type=jnp.float32)


def on_device(acts, grad_out, expert_ids, route_weights, w_gate, w_up, w_down):
    tokens, grads, ids, gain = acts[0], grad_out[0], expert_ids[0], route_weights[0]
    gate_weight, up_weight, down_weight = w_gate[0], w_up[0], w_down[0]
    count, top = ids.shape
    width = tokens.shape[1]
    units = gate_weight.shape[1]

    flat = ids.reshape(-1)
    member = (flat[:, None] == jnp.arange(CHIPS, dtype=jnp.int32)[None, :]).astype(jnp.bfloat16)
    before = jnp.tril(jnp.ones((count * top, count * top), jnp.bfloat16), -1)
    rank = jnp.sum(dot(before, member, (1, 0)) * member.astype(jnp.float32), axis=1)
    slot = (flat * CAP + rank.astype(jnp.int32)).reshape(count, top)
    hits = (slot[:, :, None] == jnp.arange(CHIPS * CAP, dtype=jnp.int32)).astype(jnp.float32)
    placing = jnp.sum(hits, axis=1).astype(jnp.bfloat16)
    high, low = split_gain(jnp.sum(hits * gain[:, :, None], axis=1))

    slot_tokens = dot(placing, tokens, (0, 0)).astype(jnp.bfloat16)
    slot_grads = (dot(high, grads, (0, 0)) + dot(low, grads, (0, 0))).astype(jnp.bfloat16)
    rows_in, rows_grad = dispatch(
        slot_tokens.reshape(CHIPS, CAP, width), slot_grads.reshape(CHIPS, CAP, width)
    )
    rows_in = rows_in.reshape(2 * CHIPS * CAP, width)
    rows_grad = rows_grad.reshape(2 * CHIPS * CAP, width)

    pre_gate = dot(rows_in, gate_weight, (1, 0))
    pre_up = dot(rows_in, up_weight, (1, 0))
    hidden_grad = dot(rows_grad, down_weight, (1, 1))
    sigma = jax.nn.sigmoid(pre_gate)
    active = pre_gate * sigma
    hidden = (active * pre_up).astype(jnp.bfloat16)
    gate_grad = (hidden_grad * pre_up * sigma * (1.0 + pre_gate * (1.0 - sigma))).astype(
        jnp.bfloat16
    )
    up_grad = (hidden_grad * active).astype(jnp.bfloat16)

    pipe = lax.axis_index("pipe")
    ranks = lax.axis_size("pipe")
    half = units // 2
    kept = (pipe >= ranks // 2).astype(jnp.int32) * half
    mirror = [(p, ranks - 1 - p) for p in range(ranks)]

    def cut(array, start):
        return lax.dynamic_slice_in_dim(array, start, half, 1)

    gave = [
        lax.ppermute(part.astype(jnp.bfloat16), "pipe", mirror)
        for part in (
            dot(rows_in, cut(gate_grad, half - kept), (0, 0)),
            dot(rows_in, cut(up_grad, half - kept), (0, 0)),
            dot(cut(hidden, half - kept), rows_grad, (0, 0)),
        )
    ]

    out_part = dot(hidden, down_weight, (1, 0)).astype(jnp.bfloat16)
    input_part = (dot(gate_grad, gate_weight, (1, 1)) + dot(up_grad, up_weight, (1, 1))).astype(
        jnp.bfloat16
    )
    back_out, back_input = give_back(
        out_part.reshape(2 * CHIPS, CAP, width), input_part.reshape(2 * CHIPS, CAP, width)
    )
    back_out = back_out.reshape(CHIPS * CAP, width)
    back_input = back_input.reshape(CHIPS * CAP, width)
    out_acts = (dot(high, back_out, (1, 0)) + dot(low, back_out, (1, 0))).astype(jnp.bfloat16)
    grad_acts = dot(placing, back_input, (1, 0)).astype(jnp.bfloat16)

    kept_parts = (
        dot(rows_in, cut(gate_grad, kept), (0, 0)),
        dot(rows_in, cut(up_grad, kept), (0, 0)),
        dot(cut(hidden, kept), rows_grad, (0, 0)),
    )
    sums = [
        (part.astype(jnp.bfloat16).astype(jnp.float32) + other.astype(jnp.float32)).astype(jnp.bfloat16)[None]
        for part, other in zip(kept_parts, gave)
    ]
    return (out_acts[None], grad_acts[None], *sums)


def solution(mesh):
    rows = P("pipe", "expert", None)
    columns = P("pipe", None, "expert")
    return jax.shard_map(
        on_device,
        mesh=mesh,
        in_specs=(rows, rows, rows, rows, columns, columns, rows),
        out_specs=(rows, rows, columns, columns, rows),
        check_vma=False,
    )
```

time: 592 us -> 303 us (0.51)
  the two profiles are of different devices: /device:TPU:96 before, /device:TPU:1 now
where the time goes in v1:
time: 303 us
  Pallas kernels  219 us (72%)
  matrix products  71 us (23%)
  starting transfers between devices  9.98 us (3%)
    pallas_call x1, Pallas kernels, give_back(): pl.pallas_call(return_kernel, name='give_back', out_shape=(shape, shape),...  147 us
    pallas_call x1, Pallas kernels, dispatch(): pl.pallas_call(dispatch_kernel, name='dispatch', out_shape=(shape, shape)...  72.2 us
    dot_general x19, matrix products, dot(): lax.dot_general(a, b, ((contract[:1], contract[1:]), ((), ())), preferred...  71 us
    ppermute x3, starting transfers between devices, on_device(): lax.ppermute(part.astype(jnp.bfloat16), 'pipe', mirror)  9.98 us
  transfers between devices with their start and end apart: 3, of which 0 were waited for; matrix products, arithmetic and copies ran while one was open for 13% of the time, Pallas kernels for 48%

profile of v1, /device:TPU:1, one launch (start us, length us, event | category | flops | bytes accessed | tf_op | source)
XLA Modules:
  0.0 303.2 jit_solution(14599542324296266993)
XLA Ops:
  0.6 0.0 copy-start
  0.7 0.9 copy.17
  1.5 0.1 eq.28
  1.7 0.3 fusion.21
  2.0 0.1 convert_element_type.107
  2.1 0.1 copy.19
  2.2 0.9 select_reduce_fusion
  3.0 0.0 copy-done
  3.1 0.9 fusion.23
  4.0 0.0 copy-start.2
  4.0 2.5 fusion
  6.5 0.0 copy-done.2
  6.5 2.5 convolution_convert_fusion.1
  8.9 72.2 %dispatch.1 = (bf16[16,48,3584]{2,1,0:T(8,128)(2,1)}, bf16[16,48,3584]{2,1,0:T(8,128)(2,1)}) custom-call(bf16[8,48,3584]{2,1,0:T(8,128)(2,1)} %bitcast.73, bf16[8,48,3584]{2,1,0:T(8,128)(2,1)} %bitcast.72), custom_call_target="tpu_custom_call" | custom-call | tf_op jit(solution)/shard_map/dispatch/pallas_call | solution.py:94
  81.2 0.0 copy-start.3
  81.2 0.0 copy-start.4
  81.2 8.0 %fusion.11 = f32[768,512]{1,0:T(8,128)} fusion(bf16[768,3584]{1,0:T(8,128)(2,1)} %bitcast.76, bf16[1,3584,512]{2,1,0:T(8,128)(2,1)} %param.12), kind=kOutput, calls=%fused_computation.23 | convolution fusion | flops 2818572288 | bytes 10747904 | tf_op jit(solution)/shard_map/dot_general | solution.py:201
  89.1 0.0 copy-done.3
  89.1 0.0 copy-done.4
  89.1 0.0 slice-start
  89.2 4.1 %fusion.15 = f32[768,512]{1,0:T(8,128)} fusion(bf16[768,3584]{1,0:T(8,128)(2,1)S(1)} %bitcast.78, bf16[1,3584,512]{2,1,0:T(8,128)(2,1)S(1)} %copy-done.4), kind=kOutput, calls=%fused_computation.27 | convolution fusion | flops 2818572288 | bytes 10747904 | tf_op jit(solution)/shard_map/dot_general | solution.py:201
  93.3 0.0 slice-start.1
  93.3 8.3 %multiply_convert_fusion = (bf16[768,512]{1,0:T(8,128)(2,1)S(1)}, bf16[768,512]{1,0:T(8,128)(2,1)S(1)}, bf16[768,512]{1,0:T(8,128)(2,1)S(1)}) fusion(f32[768,512]{1,0:T(8,128)} %fusion.15, f32[768,512]{1,0:T(8,128)} %fusion.11, bf16[768,3584]{1,0:T(8,128)(2,1)} %bitcast.67, bf16[1,512,3584]{2,1,0:T(8,128)(2,1)} %param.13), kind=kOutput, calls=%fused_computation.35 | convolution fusion | flops 2824470528 | bytes 14680064 | tf_op jit(solution)/shard_map/dot_general | solution.py:201
  101.6 0.0 slice-done
  101.6 0.0 slice-done.1
  101.6 0.0 slice-start.2
  101.6 1.6 convolution_convert_fusion.2
  103.3 4.9 %collective-permute-start.2 = (bf16[256,3584]{1,0:T(8,128)(2,1)S(1)}, bf16[256,3584]{1,0:T(8,128)(2,1)S(1)}, u32[]{:S(2)}, u32[]{:S(2)}) collective-permute-start(bf16[256,3584]{1,0:T(8,128)(2,1)S(1)} %convolution_convert_fusion.2), channel_id=1, source_target_pairs={{0,112},{16,96},{32,80},{48,64},{64,48},{80,32},{96,16},{112,0},{1... | collective-permute-start | bytes 5505032 | tf_op jit(solution)/shard_map/ppermute | solution.py:249
  108.1 0.0 slice-start.3
  108.2 5.5 %convolution_convert_fusion.4 = bf16[3584,256]{1,0:T(8,128)(2,1)} fusion(bf16[768,3584]{1,0:T(8,128)(2,1)} %bitcast.77, bf16[768,512]{1,0:T(8,128)(2,1)S(1)} %get-tuple-element.15, s32[]{:T(128)S(6)} %select_n.7), kind=kOutput, calls=%fused_computation.8 | convolution fusion | flops 1410203648 | bytes 7733252 | tf_op jit(solution)/shard_map/dot_general | solution.py:201
  113.7 0.3 collective-permute-start.1
  114.0 0.0 slice-done.2
  114.0 0.0 slice-done.3
  114.0 0.0 copy-start.5
  114.0 3.0 convolution_convert_fusion.6
  116.9 0.0 copy-start.6
  116.9 4.8 %collective-permute-start = (bf16[3584,256]{1,0:T(8,128)(2,1)}, bf16[3584,256]{1,0:T(8,128)(2,1)}, u32[]{:S(2)}, u32[]{:S(2)}) collective-permute-start(bf16[3584,256]{1,0:T(8,128)(2,1)} %convolution_convert_fusion.6), channel_id=1, source_target_pairs={{0,112},{16,96},{32,80},{48,64},{64,48},{80,32},{96,16},{112,0},{1... | collective-permute-start | bytes 5505032 | tf_op jit(solution)/shard_map/ppermute | solution.py:249
  121.7 0.0 copy-done.5
  121.8 5.9 %fusion.13 = f32[768,3584]{1,0:T(8,128)} fusion(bf16[768,512]{1,0:T(8,128)(2,1)S(1)} %get-tuple-element.16, bf16[1,3584,512]{2,1,0:T(8,128)(2,1)S(1)} %copy-done.5), kind=kOutput, calls=%fused_computation.25 | convolution fusion | flops 2818572288 | bytes 15466496 | tf_op jit(solution)/shard_map/dot_general | solution.py:201
  127.6 0.0 copy-done.6
  127.6 7.4 %add_convert_fusion = bf16[768,3584]{1,0:T(8,128)(2,1)} fusion(f32[768,3584]{1,0:T(8,128)} %fusion.13, bf16[768,512]{1,0:T(8,128)(2,1)S(1)} %get-tuple-element.15, bf16[1,3584,512]{2,1,0:T(8,128)(2,1)S(1)} %copy-done.6), kind=kOutput, calls=%fused_computation | convolution fusion | flops 2824077312 | bytes 20971520 | tf_op jit(solution)/shard_map/dot_general | solution.py:201
  135.0 5.2 %convolution_convert_fusion = bf16[768,3584]{1,0:T(8,128)(2,1)S(1)} fusion(bf16[768,512]{1,0:T(8,128)(2,1)S(1)} %get-tuple-element.17, bf16[1,512,3584]{2,1,0:T(8,128)(2,1)} %param.13), kind=kOutput, calls=%fused_computation.1 | convolution fusion | flops 2821324800 | bytes 9961472 | tf_op jit(solution)/shard_map/dot_general | solution.py:201
  140.3 147.0 %give_back.1 = (bf16[8,48,3584]{2,1,0:T(8,128)(2,1)S(1)}, bf16[8,48,3584]{2,1,0:T(8,128)(2,1)S(1)}) custom-call(bf16[16,48,3584]{2,1,0:T(8,128)(2,1)S(1)} %bitcast.65, bf16[16,48,3584]{2,1,0:T(8,128)(2,1)} %bitcast.74), custom_call_target="tpu_custom_call" | custom-call | tf_op jit(solution)/shard_map/give_back/pallas_call | solution.py:182
  287.3 1.6 fusion.5
  288.9 0.6 fusion.53
  289.6 0.0 slice-start.4
  289.6 1.6 fusion.6
  291.2 0.0 slice-start.5
  291.2 0.0 collective-permute-done.2
  291.2 2.9 fusion.19
  294.1 0.0 collective-permute-done.1
  294.1 0.0 slice-done.4
  294.1 0.0 slice-done.5
  294.1 0.0 copy-start.1
  294.1 4.6 %fusion.18 = bf16[1,3584,256]{2,1,0:T(8,128)(2,1)} fusion(bf16[3584,256]{1,0:T(8,128)(2,1)} %collective-permute-done.1, bf16[768,3584]{1,0:T(8,128)(2,1)S(1)} %bitcast.84, bf16[768,512]{1,0:T(8,128)(2,1)S(1)} %get-tuple-element.15, s32[]{:T(128)S(6)} %mul.64), kind=kOutput, calls=%fused_computation.33 | convolution fusion | flops 1413873664 | bytes 9568260 | tf_op jit(solution)/shard_map/dot_general | solution.py:201
  298.7 0.0 collective-permute-done
  298.7 4.5 %fusion.17 = bf16[1,3584,256]{2,1,0:T(8,128)(2,1)} fusion(bf16[3584,256]{1,0:T(8,128)(2,1)} %collective-permute-done, bf16[768,3584]{1,0:T(8,128)(2,1)S(1)} %bitcast.85, bf16[768,512]{1,0:T(8,128)(2,1)S(1)} %get-tuple-element.16, s32[]{:T(128)S(6)} %mul.64), kind=kOutput, calls=%fused_computation.32 | convolution fusion | flops 1413873664 | bytes 9568260 | tf_op jit(solution)/shard_map/dot_general | solution.py:201
  303.2 0.0 copy-done.1
  (6 shorter events, 0.0 us)
Async XLA Ops:
  0.6 2.4 copy-start
  4.0 2.5 copy-start.2
  81.2 8.0 %copy-start.3 = (bf16[16,48,3584]{2,1,0:T(8,128)(2,1)S(1)}, bf16[16,48,3584]{2,1,0:T(8,128)(2,1)}, u32[]{:S(2)}) copy-start(bf16[16,48,3584]{2,1,0:T(8,128)(2,1)} %get-tuple-element.9) | copy-start | bytes 16515076
  81.2 8.0 %copy-start.4 = (bf16[1,3584,512]{2,1,0:T(8,128)(2,1)S(1)}, bf16[1,3584,512]{2,1,0:T(8,128)(2,1)}, u32[]{:S(2)}) copy-start(bf16[1,3584,512]{2,1,0:T(8,128)(2,1)} %param.11) | copy-start | bytes 11010052
  89.1 12.4 %slice-start = ((s8[5505024]{0:T(1024)(128)(4,1)}), s8[1310720]{0:T(1024)(128)(4,1)S(1)}, s32[]{:S(2)}) async-start(s8[5505024]{0:T(1024)(128)(4,1)} %bitcast.68), calls=%async_computation | async-start | bytes 2621440
  93.3 8.3 %slice-start.1 = ((s8[5505024]{0:T(1024)(128)(4,1)}), s8[4194304]{0:T(1024)(128)(4,1)S(1)}, s32[]{:S(2)}) async-start(s8[5505024]{0:T(1024)(128)(4,1)} %bitcast.68), calls=%async_computation.1 | async-start | bytes 8388608
  101.6 12.4 %slice-start.2 = ((s8[5505024]{0:T(1024)(128)(4,1)}), s8[4194304]{0:T(1024)(128)(4,1)S(1)}, s32[]{:S(2)}) async-start(s8[5505024]{0:T(1024)(128)(4,1)} %bitcast.79), calls=%async_computation.2 | async-start | bytes 8388608
  103.3 187.9 %collective-permute-start.2 = (bf16[256,3584]{1,0:T(8,128)(2,1)S(1)}, bf16[256,3584]{1,0:T(8,128)(2,1)S(1)}, u32[]{:S(2)}, u32[]{:S(2)}) collective-permute-start(bf16[256,3584]{1,0:T(8,128)(2,1)S(1)} %convolution_convert_fusion.2), channel_id=1, source_target_pairs={{0,112},{16,96},{32,80},{48,64},{64,48},{80,32},{96,16},{112,0},{1... | collective-permute-start | bytes 5505032 | tf_op jit(solution)/shard_map/ppermute | solution.py:249
  108.1 5.8 %slice-start.3 = ((s8[5505024]{0:T(1024)(128)(4,1)}), s8[1310720]{0:T(1024)(128)(4,1)S(1)}, s32[]{:S(2)}) async-start(s8[5505024]{0:T(1024)(128)(4,1)} %bitcast.79), calls=%async_computation.3 | async-start | bytes 2621440
  113.7 180.4 %collective-permute-start.1 = (bf16[3584,256]{1,0:T(8,128)(2,1)}, bf16[3584,256]{1,0:T(8,128)(2,1)}, u32[]{:S(2)}, u32[]{:S(2)}) collective-permute-start(bf16[3584,256]{1,0:T(8,128)(2,1)} %convolution_convert_fusion.4), channel_id=1, source_target_pairs={{0,112},{16,96},{32,80},{48,64},{64,48},{80,32},{96,16},{112,0},{1... | collective-permute-start | bytes 5505032 | tf_op jit(solution)/shard_map/ppermute | solution.py:249
  114.0 7.8 %copy-start.5 = (bf16[1,3584,512]{2,1,0:T(8,128)(2,1)S(1)}, bf16[1,3584,512]{2,1,0:T(8,128)(2,1)}, u32[]{:S(2)}) copy-start(bf16[1,3584,512]{2,1,0:T(8,128)(2,1)} %param.11) | copy-start | bytes 11010052
  116.9 10.7 %copy-start.6 = (bf16[1,3584,512]{2,1,0:T(8,128)(2,1)S(1)}, bf16[1,3584,512]{2,1,0:T(8,128)(2,1)}, u32[]{:S(2)}) copy-start(bf16[1,3584,512]{2,1,0:T(8,128)(2,1)} %param.12) | copy-start | bytes 11010052
  116.9 181.8 %collective-permute-start = (bf16[3584,256]{1,0:T(8,128)(2,1)}, bf16[3584,256]{1,0:T(8,128)(2,1)}, u32[]{:S(2)}, u32[]{:S(2)}) collective-permute-start(bf16[3584,256]{1,0:T(8,128)(2,1)} %convolution_convert_fusion.6), channel_id=1, source_target_pairs={{0,112},{16,96},{32,80},{48,64},{64,48},{80,32},{96,16},{112,0},{1... | collective-permute-start | bytes 5505032 | tf_op jit(solution)/shard_map/ppermute | solution.py:249
  289.6 4.5 %slice-start.4 = ((s8[5505024]{0:T(1024)(128)(4,1)}), s8[1310720]{0:T(1024)(128)(4,1)S(1)}, s32[]{:S(2)}) async-start(s8[5505024]{0:T(1024)(128)(4,1)} %bitcast.82), calls=%async_computation.4 | async-start | bytes 2621440
  291.2 2.9 slice-start.5
  294.1 9.2 %copy-start.1 = (bf16[1,128,3584]{2,1,0:T(8,128)(2,1)S(1)}, bf16[1,128,3584]{2,1,0:T(8,128)(2,1)}, u32[]{:S(2)}) copy-start(bf16[1,128,3584]{2,1,0:T(8,128)(2,1)} %param.8) | copy-start | bytes 2752516

commit v2 on v1

v2 whole, which is shorter than its diff:
```python
import functools

import jax
import jax.numpy as jnp
from jax import lax
from jax.experimental import pallas as pl
from jax.experimental.pallas import tpu as pltpu
from jax.sharding import PartitionSpec as P

MESH = pl.DeviceIdType.MESH
CHIPS = 8
CAP = 48


def place():
    pipe = lax.axis_index("pipe")
    own = lax.axis_index("expert")
    return pipe, own, own // 8, (own // 2) % 4, own % 2


def chip_at(y, z, k, sign):
    return ((y + k // 4) % 2) * 4 + (z + 4 + sign * (k % 4)) % 4


def split_gain(gain):
    high = lax.reduce_precision(gain, exponent_bits=8, mantissa_bits=7)
    low = lax.reduce_precision(gain - high, exponent_bits=8, mantissa_bits=7)
    return high.astype(jnp.bfloat16), low.astype(jnp.bfloat16)


def dot(a, b, contract):
    dims = ((contract[:1], contract[1:]), ((), ()))
    return lax.dot_general(a, b, dims, preferred_element_type=jnp.float32)


def forward_kernel(
    tokens,
    grads,
    packing,
    away_weight,
    w_gate,
    w_up,
    w_down,
    got_in,
    got_grad,
    relay_weight,
    hidden,
    gate_grad,
    up_grad,
    out_part,
    slots,
    rows,
    gate,
    up,
    down,
    pre,
    out,
    send_sem,
    recv_sem,
    near_send,
    near_recv,
    load_sem,
    keep_sem,
    out_sem,
    away_sem,
):
    pipe, own, y, z, core = place()
    chip = own // 2
    sibling = own + 1 - 2 * core
    width = tokens.shape[1]
    units = hidden.shape[1]
    step = width // 7
    group = CHIPS * CAP

    barrier = pltpu.get_barrier_semaphore()
    for k in range(1, CHIPS):
        peer = chip_at(y, z, k, 1) * 2 + core
        pl.semaphore_signal(barrier, inc=1, device_id=(pipe, peer), device_id_type=MESH)
    pl.semaphore_signal(barrier, inc=1, device_id=(pipe, sibling), device_id_type=MESH)

    loads = [
        pltpu.make_async_copy(source, target, load_sem.at[i])
        for i, (source, target) in enumerate(((w_gate, gate), (w_up, up), (w_down, down)))
    ]

    def far(a, k):
        dest = chip_at(y, z, k, 1)
        return pltpu.make_async_remote_copy(
            src_ref=slots.at[a, dest],
            dst_ref=rows.at[a, own],
            send_sem=send_sem.at[a, k],
            recv_sem=recv_sem.at[a, k],
            device_id=(pipe, dest * 2 + core),
            device_id_type=MESH,
        )

    def near(a, k):
        origin = chip_at(y, z, k, -1) * 2 + core
        return pltpu.make_async_remote_copy(
            src_ref=slots.at[a, chip] if k == 0 else rows.at[a, origin],
            dst_ref=rows.at[a, origin],
            send_sem=near_send.at[a, k],
            recv_sem=near_recv.at[a, k],
            device_id=(pipe, sibling),
            device_id_type=MESH,
        )

    away = pltpu.make_async_remote_copy(
        src_ref=away_weight,
        dst_ref=relay_weight,
        send_sem=away_sem.at[0],
        recv_sem=away_sem.at[1],
        device_id=(pipe, (own + CHIPS) % (2 * CHIPS)),
        device_id_type=MESH,
    )
    keeps = [
        pltpu.make_async_copy(rows.at[a], target, keep_sem.at[a])
        for a, target in enumerate((got_in, got_grad))
    ]

    def pack(a):
        def tile(j, carry):
            columns = pl.ds(pl.multiple_of(j * step, step), step)
            if a == 0:
                total = dot(packing[2], tokens[:, columns], (1, 0))
            else:
                part = grads[:, columns]
                total = dot(packing[0], part, (1, 0)) + dot(packing[1], part, (1, 0))
            slots[a, :, :, columns] = total.astype(jnp.bfloat16).reshape(CHIPS, CAP, step)
            return carry

        lax.fori_loop(0, 7, tile, 0)

    def send(a):
        for k in (6, 2, 5, 7, 1, 3, 4):
            far(a, k).start()
        near(a, 0).start()
        rows[a, own] = slots[a, chip]

    def receive(a):
        for k in (4, 1, 3, 5, 7, 2, 6):
            far(a, k).wait_recv()
            near(a, k).start()
        for k in range(CHIPS):
            near(a, k).wait_recv()
        keeps[a].start()

    pack(0)
    pl.semaphore_wait(barrier, CHIPS)
    send(0)
    away.start()
    for load in loads:
        load.start()
    pack(1)
    send(1)
    receive(0)
    for load in loads:
        load.wait()

    def first(i, carry):
        block = rows[0, pl.ds(i * CHIPS, CHIPS)].reshape(group, width)
        here = pl.ds(pl.multiple_of(i * group, group), group)
        for j in range(units // 256):
            some = slice(j * 256, j * 256 + 256)
            pre_gate = dot(block, gate[:, some], (1, 0))
            pre_up = dot(block, up[:, some], (1, 0))
            pre[0, here, some] = pre_gate
            pre[1, here, some] = pre_up
            hidden[here, some] = (pre_gate * jax.nn.sigmoid(pre_gate) * pre_up).astype(jnp.bfloat16)
        return carry

    lax.fori_loop(0, 2, first, 0)

    def second(j, carry):
        columns = pl.ds(pl.multiple_of(j * step, step), step)
        for i in range(2):
            part = dot(hidden[i * group : i * group + group, :], down[:, columns], (1, 0))
            out[i * CHIPS : i * CHIPS + CHIPS, :, columns] = part.astype(jnp.bfloat16).reshape(
                CHIPS, CAP, step
            )
        return carry

    lax.fori_loop(0, 7, second, 0)
    store = pltpu.make_async_copy(out, out_part, out_sem.at[0])
    store.start()

    receive(1)

    def third(i, carry):
        block = rows[1, pl.ds(i * CHIPS, CHIPS)].reshape(group, width)
        here = pl.ds(pl.multiple_of(i * group, group), group)
        for j in range(units // 256):
            some = slice(j * 256, j * 256 + 256)
            hidden_grad = dot(block, down[some, :], (1, 1))
            pre_gate = pre[0, here, some]
            sigma = jax.nn.sigmoid(pre_gate)
            slope = sigma * (1.0 + pre_gate * (1.0 - sigma))
            gate_grad[here, some] = (hidden_grad * pre[1, here, some] * slope).astype(jnp.bfloat16)
            up_grad[here, some] = (hidden_grad * (pre_gate * sigma)).astype(jnp.bfloat16)
        return carry

    lax.fori_loop(0, 2, third, 0)

    store.wait()
    away.wait()
    for a in range(2):
        keeps[a].wait()
        for k in range(CHIPS):
            near(a, k).wait_send()
            if k:
                far(a, k).wait_send()


def forward(tokens, grads, packing, away_weight, w_gate, w_up, w_down):
    width = tokens.shape[1]
    units = w_gate.shape[1]
    anywhere = pl.BlockSpec(memory_space=pl.ANY)
    vmem = pl.BlockSpec(memory_space=pltpu.VMEM)
    dma = pltpu.SemaphoreType.DMA
    kind = tokens.dtype
    blocks = (2 * CHIPS, CAP, width)
    count = 2 * CHIPS * CAP
    many = jax.ShapeDtypeStruct(blocks, kind)
    inner = jax.ShapeDtypeStruct((count, units), kind)
    return pl.pallas_call(
        forward_kernel,
        name="forward",
        out_shape=(
            many,
            many,
            jax.ShapeDtypeStruct(away_weight.shape, kind),
            inner,
            inner,
            inner,
            many,
        ),
        in_specs=[vmem] * 3 + [anywhere] * 4,
        out_specs=(anywhere, anywhere, anywhere, vmem, vmem, vmem, anywhere),
        scratch_shapes=[
            pltpu.VMEM((2, CHIPS, CAP, width), kind),
            pltpu.VMEM((2, *blocks), kind),
            pltpu.VMEM(w_gate.shape, kind),
            pltpu.VMEM(w_up.shape, kind),
            pltpu.VMEM(w_down.shape, kind),
            pltpu.VMEM((2, count, units), jnp.float32),
            pltpu.VMEM(blocks, kind),
        ]
        + [dma((2, CHIPS))] * 4
        + [dma((3,)), dma((2,)), dma((1,)), dma((2,))],
        compiler_params=pltpu.CompilerParams(
            collective_id=1, has_side_effects=True, vmem_limit_bytes=58 << 20
        ),
    )(tokens, grads, packing, away_weight, w_gate, w_up, w_down)


def return_kernel(
    out_part,
    input_part,
    own_weight,
    relay_weight,
    out_acts,
    grad_acts,
    halves,
    mine,
    sums,
    landing,
    partial,
    remote,
    near_send,
    near_recv,
    mine_sem,
    send_sem,
    recv_sem,
    across_send,
    across_recv,
):
    pipe, own, y, z, core = place()
    arrays = (out_part, input_part)
    results = (out_acts, grad_acts)
    sibling = own + 1 - 2 * core
    opposite = (own + CHIPS) % (2 * CHIPS)

    barrier = pltpu.get_barrier_semaphore()
    for peer in [(y * 4 + (z + dz) % 4) * 2 + core for dz in range(1, 4)] + [sibling, opposite]:
        pl.semaphore_signal(barrier, inc=1, device_id=(pipe, peer), device_id_type=MESH)
    pl.semaphore_wait(barrier, 5)

    def near(a, k):
        there = chip_at(y, z, k, 1) * 2 + 1 - core
        return pltpu.make_async_remote_copy(
            src_ref=arrays[a].at[there],
            dst_ref=halves.at[a, k],
            send_sem=near_send.at[a, k],
            recv_sem=near_recv.at[a, k],
            device_id=(pipe, sibling),
            device_id_type=MESH,
        )

    def load(a, k):
        here = chip_at(y, z, k, 1) * 2 + core
        return pltpu.make_async_copy(arrays[a].at[here], mine.at[a, k], mine_sem.at[a, k])

    def along(a, k):
        return pltpu.make_async_remote_copy(
            src_ref=sums.at[a, k],
            dst_ref=landing.at[a, k // 4, z],
            send_sem=send_sem.at[a, k],
            recv_sem=recv_sem.at[a, k],
            device_id=(pipe, (y * 4 + (z + k % 4) % 4) * 2 + core),
            device_id_type=MESH,
        )

    def across(a):
        return pltpu.make_async_remote_copy(
            src_ref=partial.at[a],
            dst_ref=remote.at[a],
            send_sem=across_send.at[a],
            recv_sem=across_recv.at[a],
            device_id=(pipe, opposite),
            device_id_type=MESH,
        )

    width = out_acts.shape[1]
    step = width // 7

    def combine(a, dy, weight, put):
        for k in range(4 * dy + 1, 4 * dy + 4):
            along(a, k).wait_recv()

        def tile(j, carry):
            columns = pl.ds(pl.multiple_of(j * step, step), step)
            rows = landing[a, dy, :, :, columns].reshape(4 * CAP, step)
            if a == 0:
                total = jnp.dot(weight[0], rows, preferred_element_type=jnp.float32)
                total += jnp.dot(weight[1], rows, preferred_element_type=jnp.float32)
            else:
                total = jnp.dot(weight[2], rows, preferred_element_type=jnp.float32)
            put(columns, total)
            return carry

        lax.fori_loop(0, width // step, tile, 0)

    order = [(a, 4 * dy + dz) for dy in (1, 0) for a in range(2) for dz in (2, 1, 3, 0)]
    for a, k in order:
        near(a, k).start()
        load(a, k).start()
    for a, k in order:
        load(a, k).wait()
        near(a, k).wait_recv()
        total = halves[a, k].astype(jnp.float32) + mine[a, k].astype(jnp.float32)
        if k % 4:
            sums[a, k] = total.astype(jnp.bfloat16)
            along(a, k).start()
        else:
            landing[a, k // 4, z] = total.astype(jnp.bfloat16)
    for a in range(2):

        def send_on(columns, total, a=a):
            partial[a, :, columns] = total.astype(jnp.bfloat16)

        combine(a, 1, relay_weight, send_on)
        across(a).start()
    for a in range(2):
        across(a).wait_recv()

        def finish(columns, total, a=a):
            total = total + remote[a, :, columns].astype(jnp.float32)
            results[a][:, columns] = total.astype(jnp.bfloat16)

        combine(a, 0, own_weight, finish)
    for a in range(2):
        across(a).wait_send()
        for k in range(CHIPS):
            near(a, k).wait_send()
            if k % 4:
                along(a, k).wait_send()


def give_back(out_part, input_part, own_weight, relay_weight):
    width = out_part.shape[-1]
    count = own_weight.shape[1]
    anywhere = pl.BlockSpec(memory_space=pl.ANY)
    vmem = pl.BlockSpec(memory_space=pltpu.VMEM)
    dma = pltpu.SemaphoreType.DMA
    shape = jax.ShapeDtypeStruct((count, width), out_part.dtype)
    block = pltpu.VMEM((2, CHIPS, CAP, width), out_part.dtype)
    sent = pltpu.VMEM((2, count, width), out_part.dtype)
    return pl.pallas_call(
        return_kernel,
        name="give_back",
        out_shape=(shape, shape),
        in_specs=[anywhere, anywhere, vmem, vmem],
        out_specs=(vmem, vmem),
        scratch_shapes=[block] * 3
        + [pltpu.VMEM((2, 2, 4, CAP, width), out_part.dtype), sent, sent]
        + [dma((2, CHIPS))] * 5
        + [dma((2,))] * 2,
        compiler_params=pltpu.CompilerParams(
            collective_id=2, has_side_effects=True, vmem_limit_bytes=48 << 20
        ),
    )(out_part, input_part, own_weight, relay_weight)


def on_device(acts, grad_out, expert_ids, route_weights, w_gate, w_up, w_down):
    tokens, grads, ids, gain = acts[0], grad_out[0], expert_ids[0], route_weights[0]
    gate_weight, up_weight, down_weight = w_gate[0], w_up[0], w_down[0]
    count, top = ids.shape
    width = tokens.shape[1]
    units = gate_weight.shape[1]

    flat = ids.reshape(-1)
    member = (flat[:, None] == jnp.arange(CHIPS, dtype=jnp.int32)[None, :]).astype(jnp.bfloat16)
    before = jnp.tril(jnp.ones((count * top, count * top), jnp.bfloat16), -1)
    rank = jnp.sum(dot(before, member, (1, 0)) * member.astype(jnp.float32), axis=1)
    slot = (flat * CAP + rank.astype(jnp.int32)).reshape(count, top)
    hits = (slot[:, :, None] == jnp.arange(CHIPS * CAP, dtype=jnp.int32)).astype(jnp.float32)
    placing = jnp.sum(hits, axis=1).astype(jnp.bfloat16)
    high, low = split_gain(jnp.sum(hits * gain[:, :, None], axis=1))

    weights = jnp.stack([high, low, placing])
    side = lax.axis_index("expert") // CHIPS
    own_weight = lax.dynamic_slice_in_dim(weights, side * (4 * CAP), 4 * CAP, 2)
    away_weight = lax.dynamic_slice_in_dim(weights, (1 - side) * (4 * CAP), 4 * CAP, 2)
    packing = weights.swapaxes(1, 2)
    rows_in, rows_grad, relay_weight, hidden, gate_grad, up_grad, out_part = forward(
        tokens, grads, packing, away_weight, gate_weight, up_weight, down_weight
    )
    rows_in = rows_in.reshape(2 * CHIPS * CAP, width)
    rows_grad = rows_grad.reshape(2 * CHIPS * CAP, width)

    pipe = lax.axis_index("pipe")
    ranks = lax.axis_size("pipe")
    half = units // 2
    kept = (pipe >= ranks // 2).astype(jnp.int32) * half
    mirror = [(p, ranks - 1 - p) for p in range(ranks)]

    def cut(array, start):
        return lax.dynamic_slice_in_dim(array, start, half, 1)

    gave = [
        lax.ppermute(part.astype(jnp.bfloat16), "pipe", mirror)
        for part in (
            dot(rows_in, cut(gate_grad, half - kept), (0, 0)),
            dot(rows_in, cut(up_grad, half - kept), (0, 0)),
            dot(cut(hidden, half - kept), rows_grad, (0, 0)),
        )
    ]

    input_part = (dot(gate_grad, gate_weight, (1, 1)) + dot(up_grad, up_weight, (1, 1))).astype(
        jnp.bfloat16
    )
    kept_parts = [
        part.astype(jnp.bfloat16)
        for part in (
            dot(rows_in, cut(gate_grad, kept), (0, 0)),
            dot(rows_in, cut(up_grad, kept), (0, 0)),
            dot(cut(hidden, kept), rows_grad, (0, 0)),
        )
    ]
    kept_parts, out_part, input_part = lax.optimization_barrier((kept_parts, out_part, input_part))
    out_acts, grad_acts = give_back(
        out_part,
        input_part.reshape(2 * CHIPS, CAP, width),
        own_weight,
        relay_weight,
    )
    sums = [
        (part.astype(jnp.float32) + other.astype(jnp.float32)).astype(jnp.bfloat16)[None]
        for part, other in zip(kept_parts, gave)
    ]
    return (out_acts[None], grad_acts[None], *sums)


def solution(mesh):
    rows = P("pipe", "expert", None)
    columns = P("pipe", None, "expert")
    return jax.shard_map(
        on_device,
        mesh=mesh,
        in_specs=(rows, rows, rows, rows, columns, columns, rows),
        out_specs=(rows, rows, columns, columns, rows),
        check_vma=False,
    )
```

time: 303 us -> 266 us (0.88)
  matrix products: 71 us -> 32.8 us
  Pallas kernels: 219 us -> 209 us
  other arithmetic: 0.89 us -> 7.66 us
  local copies, waits for them, and re-layouts: 1.26 us -> 4.75 us
    dot_general x19 -> x9, matrix products: 71 us -> 32.8 us  [dot(): return lax.dot_general(a, b, dims, preferred_element_type=jnp.float32)]
    pallas_call x1, Pallas kernels: 147 us -> 127 us  [give_back(): pl.pallas_call(return_kernel, name='give_back', out_shape=(shape, shape),...]
    pallas_call x1, Pallas kernels: 72.2 us -> 82.4 us  [forward(): pl.pallas_call(forward_kernel, name='forward', out_shape=(many, many, jax...]
    broadcast_in_dim x0 -> x3, other arithmetic: none -> 6.68 us  [on_device(): (part.astype(jnp.float32) + other.astype(jnp.float32)).astype(jnp.bfloat16)]
  transfers between devices with their start and end apart: 3 -> 3, of which waited for: 0 -> 0; matrix products, arithmetic and copies ran while one was open for 13% -> 12% of each run, Pallas kernels for 48% -> 48%
where the time goes in v2:
time: 266 us; the launch traced here: 265 us
  Pallas kernels  209 us (79%)
  matrix products  32.8 us (12%)
  starting transfers between devices  9.96 us (4%)
  other arithmetic  7.66 us (3%)
  local copies, waits for them, and re-layouts  4.75 us (2%)
    pallas_call x1, Pallas kernels, give_back(): pl.pallas_call(return_kernel, name='give_back', out_shape=(shape, shape),...  127 us
    pallas_call x1, Pallas kernels, forward(): pl.pallas_call(forward_kernel, name='forward', out_shape=(many, many, jax...  82.4 us
    dot_general x9, matrix products, dot(): return lax.dot_general(a, b, dims, preferred_element_type=jnp.float32)  32.8 us
    ppermute x3, starting transfers between devices, on_device(): lax.ppermute(part.astype(jnp.bfloat16), 'pipe', mirror)  9.96 us
    broadcast_in_dim x3, other arithmetic, on_device(): (part.astype(jnp.float32) + other.astype(jnp.float32)).astype(jnp.bfloat16)  6.68 us
  transfers between devices with their start and end apart: 3, of which 0 were waited for; matrix products, arithmetic and copies ran while one was open for 12% of the time, Pallas kernels for 48%

profile of v2, /device:TPU:1, one launch (start us, length us, event | category | flops | bytes accessed | tf_op | source)
XLA Modules:
  0.0 265.4 jit_solution(16579233681524722869)
XLA Ops:
  0.7 0.8 copy.19
  1.5 0.1 eq.28
  1.6 0.3 fusion.3
  1.9 0.1 convert_element_type.104
  2.0 0.1 copy.21
  2.1 0.9 select_reduce_fusion
  3.0 0.1 pad_maximum_fusion
  3.1 0.9 copy.22.packing
  4.0 0.8 constant_dynamic-slice_fusion
  4.8 82.4 %forward.1 = (bf16[16,48,3584]{2,1,0:T(8,128)(2,1)}, bf16[16,48,3584]{2,1,0:T(8,128)(2,1)}, bf16[3,128,192]{2,1,0:T(8,128)(2,1)}, bf16[768,512]{1,0:T(8,128)(2,1...) custom-call(bf16[128,3584]{1,0:T(8,128)(2,1)} %bitcast.49, ...), custom_call_target="tpu_custom_call" | custom-call | tf_op jit(solution)/shard_map/forward/pallas_call | solution.py:225
  87.2 0.0 copy-start.6
  87.2 0.0 copy-start.8
  87.2 0.0 slice-start
  87.2 4.4 %convolution_convert_fusion.2 = bf16[3584,256]{1,0:T(8,128)(2,1)S(1)} fusion(bf16[768,3584]{1,0:T(8,128)(2,1)} %bitcast.53, bf16[768,512]{1,0:T(8,128)(2,1)} %get-tuple-element.20, s32[]{:T(128)S(6)} %select_n.27), kind=kOutput, calls=%fused_computation.3 | convolution fusion | flops 1410203648 | bytes 7733252 | tf_op jit(solution)/shard_map/dot_general | solution.py:33
  91.7 4.9 %collective-permute-start = (bf16[3584,256]{1,0:T(8,128)(2,1)S(1)}, bf16[3584,256]{1,0:T(8,128)(2,1)S(1)}, u32[]{:S(2)}, u32[]{:S(2)}) collective-permute-start(bf16[3584,256]{1,0:T(8,128)(2,1)S(1)} %convolution_convert_fusion.2), channel_id=1, source_target_pairs={{0,112},{16,96},{32,80},{48,64},{64,48},{80,32},{96,16},{112,0},{1... | collective-permute-start | bytes 5505032 | tf_op jit(solution)/shard_map/ppermute | solution.py:441
  96.6 0.0 copy-done.6
  96.6 0.0 copy-done.8
  96.6 0.0 slice-start.1
  96.6 0.0 copy-start.4
  96.6 3.0 %convolution_convert_fusion.1 = bf16[3584,256]{1,0:T(8,128)(2,1)} fusion(bf16[768,3584]{1,0:T(8,128)(2,1)S(1)} %bitcast.55, bf16[768,512]{1,0:T(8,128)(2,1)S(1)} %copy-done.8, s32[]{:T(128)S(6)} %select_n.27), kind=kOutput, calls=%fused_computation.2 | convolution fusion | flops 1410203648 | bytes 7733252 | tf_op jit(solution)/shard_map/dot_general | solution.py:33
  99.5 0.3 collective-permute-start.1
  99.8 0.0 slice-done
  99.8 0.0 slice-done.1
  99.8 0.0 copy-done.4
  99.8 2.9 %convolution_convert_fusion = bf16[256,3584]{1,0:T(8,128)(2,1)} fusion(bf16[768,3584]{1,0:T(8,128)(2,1)S(1)} %bitcast.43, bf16[768,512]{1,0:T(8,128)(2,1)S(1)} %copy-done.4, s32[]{:T(128)S(6)} %select_n.27), kind=kOutput, calls=%fused_computation.1 | convolution fusion | flops 1410203648 | bytes 7733252 | tf_op jit(solution)/shard_map/dot_general | solution.py:33
  102.7 0.0 copy-start.1
  102.7 0.0 copy-start.7
  102.7 4.8 %collective-permute-start.2 = (bf16[256,3584]{1,0:T(8,128)(2,1)}, bf16[256,3584]{1,0:T(8,128)(2,1)}, u32[]{:S(2)}, u32[]{:S(2)}) collective-permute-start(bf16[256,3584]{1,0:T(8,128)(2,1)} %convolution_convert_fusion), channel_id=1, source_target_pairs={{0,112},{16,96},{32,80},{48,64},{64,48},{80,32},{96,16},{112,0},{1... | collective-permute-start | bytes 5505032 | tf_op jit(solution)/shard_map/ppermute | solution.py:441
  107.5 3.0 %convolution_convert_fusion.4 = bf16[3584,256]{1,0:T(8,128)(2,1)} fusion(bf16[768,3584]{1,0:T(8,128)(2,1)S(1)} %bitcast.56, bf16[768,512]{1,0:T(8,128)(2,1)S(1)} %copy-done.8, s32[]{:T(128)S(6)} %mul.43), kind=kOutput, calls=%fused_computation.5 | convolution fusion | flops 1410203648 | bytes 7733252 | tf_op jit(solution)/shard_map/dot_general | solution.py:33
  110.4 0.0 copy-done.1
  110.4 0.0 copy-done.7
  110.4 0.0 copy-start.2
  110.5 5.8 %fusion.26 = f32[768,3584]{1,0:T(8,128)} fusion(bf16[768,512]{1,0:T(8,128)(2,1)S(1)} %copy-done.7, bf16[1,3584,512]{2,1,0:T(8,128)(2,1)S(1)} %copy-done.1), kind=kOutput, calls=%fused_computation.49 | convolution fusion | flops 2818572288 | bytes 15466496 | tf_op jit(solution)/shard_map/dot_general | solution.py:33
  116.2 0.0 copy-done.2
  116.2 0.0 copy-start.5
  116.2 7.7 %add_convert_fusion = bf16[768,3584]{1,0:T(8,128)(2,1)} fusion(f32[768,3584]{1,0:T(8,128)} %fusion.26, bf16[768,512]{1,0:T(8,128)(2,1)} %get-tuple-element.21, bf16[1,3584,512]{2,1,0:T(8,128)(2,1)S(1)} %copy-done.2), kind=kOutput, calls=%fused_computation | convolution fusion | flops 2824077312 | bytes 20971520 | tf_op jit(solution)/shard_map/dot_general | solution.py:33
  123.9 0.0 copy-done.5
  123.9 1.6 convolution_convert_fusion.3
  125.6 0.0 copy-start
  125.6 4.3 %convolution_convert_fusion.5 = bf16[3584,256]{1,0:T(8,128)(2,1)S(1)} fusion(bf16[768,3584]{1,0:T(8,128)(2,1)} %bitcast.54, bf16[768,512]{1,0:T(8,128)(2,1)S(1)} %copy-done.7, s32[]{:T(128)S(6)} %mul.43), kind=kOutput, calls=%fused_computation.6 | convolution fusion | flops 1410203648 | bytes 7733252 | tf_op jit(solution)/shard_map/dot_general | solution.py:33
  129.8 0.0 copy-done
  129.8 127.0 %give_back.1 = (bf16[128,3584]{1,0:T(8,128)(2,1)S(1)}, bf16[128,3584]{1,0:T(8,128)(2,1)S(1)}) custom-call(bf16[16,48,3584]{2,1,0:T(8,128)(2,1)} %get-tuple-element.25.out_part, bf16[16,48,3584]{2,1,0:T(8,128)(2,1)} %bitcast.45, bf16[3,128,192]{2,1,0:T(8,128)(2,1)S(1)} %get-tuple-element.35.own_weight, bf16[3,128,192]{2,1,0:T(8,128)(2,1)S(1)} %copy-done), custom_call_target="tpu_custom_call" | custom-call | tf_op jit(solution)/shard_map/give_back/pallas_call | solution.py:388
  256.8 0.0 copy-start.3
  256.8 0.0 collective-permute-done.2
  256.8 3.3 %fusion.2 = bf16[1,256,3584]{2,1,0:T(8,128)(2,1)} fusion(bf16[256,3584]{1,0:T(8,128)(2,1)} %collective-permute-done.2, bf16[256,3584]{1,0:T(8,128)(2,1)S(1)} %convolution_convert_fusion.3), kind=kLoop, calls=%fused_computation.12 | loop fusion | flops 3670016 | bytes 5505024 | tf_op jit(solution)/shard_map/broadcast_in_dim | solution.py:468
  260.1 0.0 collective-permute-done.1
  260.1 0.0 copy-done.3
  260.1 1.7 fusion.1
  261.8 0.0 collective-permute-done
  261.8 1.7 fusion
  263.5 0.9 copy.25
  264.5 0.9 copy.26
  (5 shorter events, 0.0 us)
Async XLA Ops:
  87.2 9.4 %copy-start.6 = (bf16[16,48,3584]{2,1,0:T(8,128)(2,1)S(1)}, bf16[16,48,3584]{2,1,0:T(8,128)(2,1)}, u32[]{:S(2)}) copy-start(bf16[16,48,3584]{2,1,0:T(8,128)(2,1)} %get-tuple-element.19) | copy-start | bytes 16515076
  87.2 9.3 %copy-start.8 = (bf16[768,512]{1,0:T(8,128)(2,1)S(1)}, bf16[768,512]{1,0:T(8,128)(2,1)}, u32[]{:S(2)}) copy-start(bf16[768,512]{1,0:T(8,128)(2,1)} %get-tuple-element.21) | copy-start | bytes 2359300
  87.2 12.6 %slice-start = ((s8[5505024]{0:T(1024)(128)(4,1)}), s8[4194304]{0:T(1024)(128)(4,1)S(1)}, s32[]{:S(2)}) async-start(s8[5505024]{0:T(1024)(128)(4,1)} %bitcast.41), calls=%async_computation | async-start | bytes 8388608
  91.7 170.2 %collective-permute-start = (bf16[3584,256]{1,0:T(8,128)(2,1)S(1)}, bf16[3584,256]{1,0:T(8,128)(2,1)S(1)}, u32[]{:S(2)}, u32[]{:S(2)}) collective-permute-start(bf16[3584,256]{1,0:T(8,128)(2,1)S(1)} %convolution_convert_fusion.2), channel_id=1, source_target_pairs={{0,112},{16,96},{32,80},{48,64},{64,48},{80,32},{96,16},{112,0},{1... | collective-permute-start | bytes 5505032 | tf_op jit(solution)/shard_map/ppermute | solution.py:441
  96.6 3.2 %slice-start.1 = ((s8[5505024]{0:T(1024)(128)(4,1)}), s8[1310720]{0:T(1024)(128)(4,1)S(1)}, s32[]{:S(2)}) async-start(s8[5505024]{0:T(1024)(128)(4,1)} %bitcast.41), calls=%async_computation.1 | async-start | bytes 2621440
  96.6 3.2 %copy-start.4 = (bf16[768,512]{1,0:T(8,128)(2,1)S(1)}, bf16[768,512]{1,0:T(8,128)(2,1)}, u32[]{:S(2)}) copy-start(bf16[768,512]{1,0:T(8,128)(2,1)} %get-tuple-element.22) | copy-start | bytes 2359300
  99.5 160.6 %collective-permute-start.1 = (bf16[3584,256]{1,0:T(8,128)(2,1)}, bf16[3584,256]{1,0:T(8,128)(2,1)S(1)}, u32[]{:S(2)}, u32[]{:S(2)}) collective-permute-start(bf16[3584,256]{1,0:T(8,128)(2,1)} %convolution_convert_fusion.1), channel_id=1, source_target_pairs={{0,112},{16,96},{32,80},{48,64},{64,48},{80,32},{96,16},{112,0},{1... | collective-permute-start | bytes 5505032 | tf_op jit(solution)/shard_map/ppermute | solution.py:441
  102.7 7.8 %copy-start.1 = (bf16[1,3584,512]{2,1,0:T(8,128)(2,1)S(1)}, bf16[1,3584,512]{2,1,0:T(8,128)(2,1)}, u32[]{:S(2)}) copy-start(bf16[1,3584,512]{2,1,0:T(8,128)(2,1)} %param.11) | copy-start | bytes 11010052
  102.7 7.8 %copy-start.7 = (bf16[768,512]{1,0:T(8,128)(2,1)S(1)}, bf16[768,512]{1,0:T(8,128)(2,1)}, u32[]{:S(2)}) copy-start(bf16[768,512]{1,0:T(8,128)(2,1)} %get-tuple-element.20) | copy-start | bytes 2359300
  102.7 154.2 %collective-permute-start.2 = (bf16[256,3584]{1,0:T(8,128)(2,1)}, bf16[256,3584]{1,0:T(8,128)(2,1)}, u32[]{:S(2)}, u32[]{:S(2)}) collective-permute-start(bf16[256,3584]{1,0:T(8,128)(2,1)} %convolution_convert_fusion), channel_id=1, source_target_pairs={{0,112},{16,96},{32,80},{48,64},{64,48},{80,32},{96,16},{112,0},{1... | collective-permute-start | bytes 5505032 | tf_op jit(solution)/shard_map/ppermute | solution.py:441
  110.4 5.8 %copy-start.2 = (bf16[1,3584,512]{2,1,0:T(8,128)(2,1)S(1)}, bf16[1,3584,512]{2,1,0:T(8,128)(2,1)}, u32[]{:S(2)}) copy-start(bf16[1,3584,512]{2,1,0:T(8,128)(2,1)} %param.12) | copy-start | bytes 11010052
  116.2 7.7 %copy-start.5 = (bf16[768,512]{1,0:T(8,128)(2,1)S(1)}, bf16[768,512]{1,0:T(8,128)(2,1)}, u32[]{:S(2)}) copy-start(bf16[768,512]{1,0:T(8,128)(2,1)} %get-tuple-element.22) | copy-start | bytes 2359300
  125.6 4.3 %copy-start = (bf16[3,128,192]{2,1,0:T(8,128)(2,1)S(1)}, bf16[3,128,192]{2,1,0:T(8,128)(2,1)}, u32[]{:S(2)}) copy-start(bf16[3,128,192]{2,1,0:T(8,128)(2,1)} %get-tuple-element.27.relay_weight) | copy-start | bytes 442372
  256.8 3.3 %copy-start.3 = (bf16[3584,256]{1,0:T(8,128)(2,1)S(1)}, bf16[3584,256]{1,0:T(8,128)(2,1)}, u32[]{:S(2)}) copy-start(bf16[3584,256]{1,0:T(8,128)(2,1)} %convolution_convert_fusion.4) | copy-start | bytes 5505028

commit v3 on v1

v3 whole, which is shorter than its diff:
```python
import functools

import jax
import jax.numpy as jnp
from jax import lax
from jax.experimental import pallas as pl
from jax.experimental.pallas import tpu as pltpu
from jax.sharding import PartitionSpec as P

MESH = pl.DeviceIdType.MESH
CHIPS = 8
CAP = 48


def place():
    pipe = lax.axis_index("pipe")
    own = lax.axis_index("expert")
    return pipe, own, own // 8, (own // 2) % 4, own % 2


def chip_at(y, z, k, sign):
    return ((y + k // 4) % 2) * 4 + (z + 4 + sign * (k % 4)) % 4


def split_gain(gain):
    high = lax.reduce_precision(gain, exponent_bits=8, mantissa_bits=7)
    low = lax.reduce_precision(gain - high, exponent_bits=8, mantissa_bits=7)
    return high.astype(jnp.bfloat16), low.astype(jnp.bfloat16)


def dot(a, b, contract):
    dims = ((contract[:1], contract[1:]), ((), ()))
    return lax.dot_general(a, b, dims, preferred_element_type=jnp.float32)


def layer_kernel(
    tokens,
    grads,
    own_weight,
    away_weight,
    w_gate,
    w_up,
    w_down,
    out_acts,
    grad_acts,
    grad_gate,
    grad_up,
    grad_down,
    mirror_in,
    relay_weight,
    mine,
    raw,
    other,
    slots,
    rows,
    gate,
    up,
    down,
    pre,
    hidden,
    gate_grad,
    up_grad,
    factors,
    mirror_factors,
    out,
    halves,
    landing,
    other_down,
    stage,
    far_send,
    far_recv,
    near_send,
    near_recv,
    half_send,
    half_recv,
    along_send,
    along_recv,
    mirror_send,
    mirror_recv,
    pass_send,
    pass_recv,
    raw_send,
    raw_recv,
    across_send,
    across_recv,
    swap_send,
    swap_recv,
    away_sem,
    load_sem,
    stage_sem,
    result_sem,
):
    pipe, own, y, z, core = place()
    sibling = own + 1 - 2 * core
    opposite = (own + CHIPS) % (2 * CHIPS)
    ranks = lax.axis_size("pipe")
    mirrored = ranks - 1 - pipe
    kept = pipe // (ranks // 2)
    width = tokens.shape[1]
    units = w_gate.shape[1]
    step = width // 7
    group = CHIPS * CAP
    half = units // 2
    peers = [(y * 4 + (z + dz) % 4) * 2 + core for dz in range(4)]

    barrier = pltpu.get_barrier_semaphore()
    for peer in peers[1:] + [sibling, opposite]:
        pl.semaphore_signal(barrier, inc=1, device_id=(pipe, peer), device_id_type=MESH)
    pl.semaphore_signal(barrier, inc=1, device_id=(mirrored, own), device_id_type=MESH)

    loads = [
        pltpu.make_async_copy(source, target, load_sem.at[i])
        for i, (source, target) in enumerate(
            (
                (tokens, mine.at[0]),
                (grads, mine.at[1]),
                (w_gate, gate),
                (w_up, up),
                (w_down, down),
                (mirror_in, rows.at[1]),
            )
        )
    ]
    for load in loads[:5]:
        load.start()

    def origin(k):
        return chip_at(y, z, k, -1) * 2 + core

    def remote(source, target, sent, got, device):
        return pltpu.make_async_remote_copy(
            src_ref=source,
            dst_ref=target,
            send_sem=sent,
            recv_sem=got,
            device_id=device,
            device_id_type=MESH,
        )

    away = remote(away_weight, relay_weight, away_sem.at[0], away_sem.at[1], (pipe, opposite))

    def cross_raw(a):
        return remote(mine.at[a], raw.at[a], raw_send.at[a], raw_recv.at[a], (pipe, opposite))

    def far(a, k):
        dz = k % 4
        source = slots.at[a * 8 + (k // 4) * 4 + (z + dz) % 4]
        target = rows.at[a, (((y + k // 4) % 2) * 4 + z) * 2 + core]
        return remote(source, target, far_send.at[a, k], far_recv.at[a, k], (pipe, peers[dz]))

    def near(a, k):
        target = rows.at[a, origin(k)]
        source = target if k % 4 else slots.at[a * 8 + (k // 4) * 4 + z]
        return remote(source, target, near_send.at[a, k], near_recv.at[a, k], (pipe, sibling))

    def to_mirror(k):
        source = rows.at[0, origin(k)]
        target = mirror_in.at[origin(k)]
        return remote(source, target, mirror_send.at[k], mirror_recv.at[k], (mirrored, own))

    def pass_on(k):
        block = mirror_in.at[origin(k)]
        return remote(block, block, pass_send.at[k], pass_recv.at[k], (pipe, sibling))

    def swap(i):
        source = down.at[pl.ds(0, half)] if i == 2 else factors.at[i, 1 - kept]
        target = other_down if i == 2 else mirror_factors.at[i]
        return remote(source, target, swap_send.at[i], swap_recv.at[i], (mirrored, own))

    parts = (out, slots)

    def give_half(a, k):
        source = parts[a].at[chip_at(y, z, k, 1) * 2 + 1 - core]
        target = halves.at[a, k]
        return remote(source, target, half_send.at[a, k], half_recv.at[a, k], (pipe, sibling))

    def along(a, k):
        source = parts[a].at[chip_at(y, z, k, 1) * 2 + core]
        target = landing.at[a, k // 4, z]
        device = (pipe, peers[k % 4])
        return remote(source, target, along_send.at[a, k], along_recv.at[a, k], device)

    def across(a):
        return remote(
            mine.at[a], other.at[a], across_send.at[a], across_recv.at[a], (pipe, opposite)
        )

    results = [
        pltpu.make_async_copy(source, target, result_sem.at[i])
        for i, (source, target) in enumerate(
            (
                (raw.at[0], out_acts),
                (raw.at[1], grad_acts),
                (down.at[pl.ds(half, half)], grad_down),
            )
        )
    ]

    def tiles(body):
        def tile(j, carry):
            body(pl.ds(pl.multiple_of(j * step, step), step))
            return carry

        lax.fori_loop(0, 7, tile, 0)

    def pack(a, side):
        weight = relay_weight if side else own_weight
        source = raw if side else mine
        first = a * 8 + side * 4

        def tile(columns):
            part = source[a, :, columns]
            if a == 0:
                total = dot(weight[2], part, (0, 0))
            else:
                total = dot(weight[0], part, (0, 0)) + dot(weight[1], part, (0, 0))
            slots[first : first + 4, :, columns] = total.astype(jnp.bfloat16).reshape(4, CAP, step)

        tiles(tile)

    def send(a, side):
        for k in (2, 1, 3):
            far(a, 4 * side + k).start()
        near(a, 4 * side).start()
        rows[a, origin(4 * side)] = slots[a * 8 + side * 4 + z]

    def receive(a, side):
        for k in (1, 3, 2):
            far(a, 4 * side + k).wait_recv()
            near(a, 4 * side + k).start()

    def mirror(side):
        for k in range(4):
            to_mirror(4 * side + k).start()

    def settle(a):
        for k in range(CHIPS):
            near(a, k).wait_recv()

    def pass_side(side):
        for k in range(4):
            to_mirror(4 * side + k).wait_recv()
            pass_on(4 * side + k).start()

    order = [4 * dy + dz for dy in (1, 0) for dz in (2, 1, 3, 0)]

    def add_halves(a):
        for k in order:
            here = chip_at(y, z, k, 1) * 2 + core
            give_half(a, k).wait_recv()
            total = halves[a, k].astype(jnp.float32) + parts[a][here].astype(jnp.float32)
            if k % 4:
                parts[a][here] = total.astype(jnp.bfloat16)
                along(a, k).start()
            else:
                landing[a, k // 4, z] = total.astype(jnp.bfloat16)

    def combine(a, dy, weight, put):
        for k in range(4 * dy + 1, 4 * dy + 4):
            along(a, k).wait_recv()

        def tile(columns):
            block = landing[a, dy, :, :, columns].reshape(4 * CAP, step)
            if a == 0:
                total = dot(weight[0], block, (1, 0)) + dot(weight[1], block, (1, 0))
            else:
                total = dot(weight[2], block, (1, 0))
            put(columns, total)

        tiles(tile)

    loads[0].wait()
    pl.semaphore_wait(barrier, 6)
    away.start()
    cross_raw(0).start()
    pack(0, 0)
    send(0, 0)
    loads[1].wait()
    pack(1, 0)
    send(1, 0)
    cross_raw(0).wait_send()
    cross_raw(1).start()
    away.wait()
    cross_raw(0).wait_recv()
    pack(0, 1)
    send(0, 1)
    receive(0, 0)
    cross_raw(1).wait_recv()
    pack(1, 1)
    send(1, 1)
    mirror(0)
    receive(0, 1)
    mirror(1)
    settle(0)
    for load in loads[2:5]:
        load.wait()

    def units_of(i, carry):
        block = rows[0, pl.ds(i * CHIPS, CHIPS)].reshape(group, width)
        here = pl.ds(pl.multiple_of(i * group, group), group)
        for j in range(2):
            some = slice(j * half, j * half + half)
            pre_gate = dot(block, gate[:, some], (1, 0))
            pre_up = dot(block, up[:, some], (1, 0))
            pre[0, here, some] = pre_gate
            pre[1, here, some] = pre_up
            value = pre_gate * jax.nn.sigmoid(pre_gate) * pre_up
            hidden[here, some] = value.astype(jnp.bfloat16)
            factors[2, j, :, here] = value.T.astype(jnp.bfloat16)
        return carry

    lax.fori_loop(0, 2, units_of, 0)

    def out_tile(columns):
        for i in range(2):
            part = dot(hidden[i * group : i * group + group, :], down[:, columns], (1, 0))
            out[i * CHIPS : i * CHIPS + CHIPS, :, columns] = part.astype(jnp.bfloat16).reshape(
                CHIPS, CAP, step
            )

    tiles(out_tile)
    for k in order:
        give_half(0, k).start()
    receive(1, 0)
    receive(1, 1)
    settle(1)

    def grads_of(i, carry):
        block = rows[1, pl.ds(i * CHIPS, CHIPS)].reshape(group, width)
        here = pl.ds(pl.multiple_of(i * group, group), group)
        for j in range(2):
            some = slice(j * half, j * half + half)
            hidden_grad = dot(block, down[some, :], (1, 1))
            pre_gate = pre[0, here, some]
            sigma = jax.nn.sigmoid(pre_gate)
            slope = sigma * (1.0 + pre_gate * (1.0 - sigma))
            for_gate = hidden_grad * pre[1, here, some] * slope
            for_up = hidden_grad * (pre_gate * sigma)
            gate_grad[here, some] = for_gate.astype(jnp.bfloat16)
            up_grad[here, some] = for_up.astype(jnp.bfloat16)
            factors[0, j, :, here] = for_gate.T.astype(jnp.bfloat16)
            factors[1, j, :, here] = for_up.T.astype(jnp.bfloat16)
        return carry

    lax.fori_loop(0, 2, grads_of, 0)
    for i in range(2):
        swap(i).start()
    add_halves(0)

    for a in range(2):
        for k in range(CHIPS):
            near(a, k).wait_send()
            if k % 4:
                far(a, k).wait_send()

    def input_tile(columns):
        for i in range(2):
            here = slice(i * group, i * group + group)
            part = dot(gate_grad[here, :], gate[columns, :], (1, 1))
            part += dot(up_grad[here, :], up[columns, :], (1, 1))
            slots[i * CHIPS : i * CHIPS + CHIPS, :, columns] = part.astype(jnp.bfloat16).reshape(
                CHIPS, CAP, step
            )

    tiles(input_tile)
    for k in order:
        give_half(1, k).start()

    def down_tile(columns):
        block = rows[1, :, :, columns].reshape(2 * group, step)
        down[:half, columns] = dot(factors[2, 1 - kept], block, (1, 0)).astype(jnp.bfloat16)
        down[half:, columns] = dot(factors[2, kept], block, (1, 0)).astype(jnp.bfloat16)

    tiles(down_tile)
    swap(2).start()
    add_halves(1)
    pass_side(0)
    pass_side(1)

    for a in range(2):
        if a == 0:
            cross_raw(1).wait_send()

        def send_on(columns, total, a=a):
            mine[a, :, columns] = total.astype(jnp.bfloat16)

        combine(a, 1, relay_weight, send_on)
        across(a).start()

    for k in range(CHIPS):
        pass_on(k).wait_recv()
    loads[5].start()
    for i in range(2):
        swap(i).wait_recv()
    loads[5].wait()
    targets = (grad_gate, grad_up)

    def staged(j, i):
        columns = pl.ds(pl.multiple_of(j * step, step), step)
        slot = j % 2
        return pltpu.make_async_copy(
            stage.at[slot, i], targets[i].at[:, columns], stage_sem.at[slot, i]
        )

    def weight_tile(j, carry):
        columns = pl.ds(pl.multiple_of(j * step, step), step)
        mine_rows = rows[0, :, :, columns].reshape(2 * group, step)
        their_rows = rows[1, :, :, columns].reshape(2 * group, step)
        for i in range(2):

            @pl.when(j >= 2)
            def _(i=i):
                staged(j - 2, i).wait()

            total = dot(factors[i, kept], mine_rows, (1, 0))
            total += dot(mirror_factors[i], their_rows, (1, 0))
            stage[j % 2, i] = total.astype(jnp.bfloat16)
            staged(j, i).start()
        return carry

    lax.fori_loop(0, 7, weight_tile, 0)

    for a in range(2):
        across(a).wait_recv()

        def finish(columns, total, a=a):
            total = total + other[a, :, columns].astype(jnp.float32)
            raw[a, :, columns] = total.astype(jnp.bfloat16)

        combine(a, 0, own_weight, finish)
        results[a].start()
    swap(2).wait_recv()

    def down_sum(columns):
        total = down[half:, columns].astype(jnp.float32) + other_down[:, columns].astype(jnp.float32)
        down[half:, columns] = total.astype(jnp.bfloat16)

    tiles(down_sum)
    results[2].start()

    for j in (5, 6):
        for i in range(2):
            staged(j, i).wait()
    for result in results:
        result.wait()
    for i in range(3):
        swap(i).wait_send()
    for a in range(2):
        across(a).wait_send()
        for k in range(CHIPS):
            give_half(a, k).wait_send()
            if k % 4:
                along(a, k).wait_send()
    for k in range(CHIPS):
        to_mirror(k).wait_send()
        pass_on(k).wait_send()


def layer(tokens, grads, own_weight, away_weight, w_gate, w_up, w_down):
    count, width = tokens.shape
    units = w_gate.shape[1]
    half = units // 2
    anywhere = pl.BlockSpec(memory_space=pl.ANY)
    vmem = pl.BlockSpec(memory_space=pltpu.VMEM)
    dma = pltpu.SemaphoreType.DMA
    kind = tokens.dtype
    blocks = (2 * CHIPS, CAP, width)
    total = 2 * CHIPS * CAP
    ours = jax.ShapeDtypeStruct((count, width), kind)
    weight = jax.ShapeDtypeStruct((half, width), kind)
    return pl.pallas_call(
        layer_kernel,
        name="layer",
        out_shape=(ours, ours, weight, weight, weight, jax.ShapeDtypeStruct(blocks, kind)),
        in_specs=[anywhere] * 2 + [vmem] + [anywhere] * 4,
        out_specs=(anywhere,) * 6,
        scratch_shapes=[
            pltpu.VMEM(own_weight.shape, kind),
            pltpu.VMEM((2, count, width), kind),
            pltpu.VMEM((2, count, width), kind),
            pltpu.VMEM((2, count, width), kind),
            pltpu.VMEM(blocks, kind),
            pltpu.VMEM((2, *blocks), kind),
            pltpu.VMEM(w_gate.shape, kind),
            pltpu.VMEM(w_up.shape, kind),
            pltpu.VMEM(w_down.shape, kind),
            pltpu.VMEM((2, total, units), jnp.float32),
            pltpu.VMEM((total, units), kind),
            pltpu.VMEM((total, units), kind),
            pltpu.VMEM((total, units), kind),
            pltpu.VMEM((3, 2, half, total), kind),
            pltpu.VMEM((2, half, total), kind),
            pltpu.VMEM(blocks, kind),
            pltpu.VMEM((2, CHIPS, CAP, width), kind),
            pltpu.VMEM((2, 2, 4, CAP, width), kind),
            pltpu.VMEM((half, width), kind),
            pltpu.VMEM((2, 2, half, width // 7), kind),
        ]
        + [dma((2, CHIPS))] * 8
        + [dma((CHIPS,))] * 4
        + [dma((2,))] * 4
        + [dma((3,))] * 2
        + [dma((2,)), dma((6,)), dma((2, 2)), dma((3,))],
        compiler_params=pltpu.CompilerParams(
            collective_id=1, has_side_effects=True, vmem_limit_bytes=62 << 20
        ),
    )(tokens, grads, own_weight, away_weight, w_gate, w_up, w_down)[:5]


def on_device(acts, grad_out, expert_ids, route_weights, w_gate, w_up, w_down):
    tokens, grads, ids, gain = acts[0], grad_out[0], expert_ids[0], route_weights[0]
    gate_weight, up_weight, down_weight = w_gate[0], w_up[0], w_down[0]
    count, top = ids.shape
    width = tokens.shape[1]
    units = gate_weight.shape[1]

    flat = ids.reshape(-1)
    member = (flat[:, None] == jnp.arange(CHIPS, dtype=jnp.int32)[None, :]).astype(jnp.bfloat16)
    before = jnp.tril(jnp.ones((count * top, count * top), jnp.bfloat16), -1)
    rank = jnp.sum(dot(before, member, (1, 0)) * member.astype(jnp.float32), axis=1)
    slot = (flat * CAP + rank.astype(jnp.int32)).reshape(count, top)
    hits = (slot[:, :, None] == jnp.arange(CHIPS * CAP, dtype=jnp.int32)).astype(jnp.float32)
    placing = jnp.sum(hits, axis=1).astype(jnp.bfloat16)
    high, low = split_gain(jnp.sum(hits * gain[:, :, None], axis=1))

    weights = jnp.stack([high, low, placing])
    side = lax.axis_index("expert") // CHIPS
    own_weight = lax.dynamic_slice_in_dim(weights, side * (4 * CAP), 4 * CAP, 2)
    away_weight = lax.dynamic_slice_in_dim(weights, (1 - side) * (4 * CAP), 4 * CAP, 2)
    out_acts, grad_acts, grad_gate, grad_up, grad_down = layer(
        tokens, grads, own_weight, away_weight, gate_weight, up_weight, down_weight
    )
    return (out_acts[None], grad_acts[None], grad_gate.T[None], grad_up.T[None], grad_down[None])


def solution(mesh):
    rows = P("pipe", "expert", None)
    columns = P("pipe", None, "expert")
    return jax.shard_map(
        on_device,
        mesh=mesh,
        in_specs=(rows, rows, rows, rows, columns, columns, rows),
        out_specs=(rows, rows, columns, columns, rows),
        check_vma=False,
    )
```

time: 303 us -> 230 us (0.76)
  matrix products: 71 us -> 0.27 us
  local copies, waits for them, and re-layouts: 1.26 us -> 12.7 us
  starting transfers between devices: 9.98 us -> 0 us
  Pallas kernels: 219 us -> 215 us
    dot_general x19 -> x1, matrix products: 71 us -> 0.27 us  [dot(): return lax.dot_general(a, b, dims, preferred_element_type=jnp.float32)]
    unnamed x27 -> x12, local copies, waits for them, and re-layouts: 0.93 us -> 11.4 us
    ppermute x3 -> x0, starting transfers between devices: 9.98 us -> none  [on_device(): lax.ppermute(part.astype(jnp.bfloat16), 'pipe', mirror)]
    pallas_call x2 -> x1, Pallas kernels: 219 us -> 215 us  [layer(): pl.pallas_call(layer_kernel, name='layer', out_shape=(ours, ours, weight,...]
  transfers between devices with their start and end apart: 3 -> 0, of which waited for: 0 -> 0; matrix products, arithmetic and copies ran while one was open for 13% -> 0% of each run, Pallas kernels for 48% -> 0%
where the time goes in v3:
time: 230 us
  Pallas kernels  215 us (93%)
  local copies, waits for them, and re-layouts  12.7 us (6%)
    pallas_call x1, Pallas kernels, layer(): pl.pallas_call(layer_kernel, name='layer', out_shape=(ours, ours, weight,...  215 us
    unnamed x12, local copies, waits for them, and re-layouts  11.4 us

profile of v3, /device:TPU:1, one launch (start us, length us, event | category | flops | bytes accessed | tf_op | source)
XLA Modules:
  0.0 229.5 jit_solution(5032643660736821563)
XLA Ops:
  0.7 0.8 copy.21
  1.5 0.1 eq.28
  1.6 0.3 fusion
  1.9 0.1 convert_element_type.55
  2.0 0.1 copy.23
  2.1 0.9 select_reduce_fusion
  3.1 0.9 constant_dynamic-slice_fusion
  4.0 214.9 %layer.1 = (bf16[128,3584]{1,0:T(8,128)(2,1)}, bf16[128,3584]{1,0:T(8,128)(2,1)}, bf16[256,3584]{1,0:T(8,128)(2,1)}, bf16[256,3584]{1,0:T(8,128)(2,1)}, bf16[256...) custom-call(bf16[128,3584]{1,0:T(8,128)(2,1)} %bitcast.29, bf16[128,3584]{1,0:T(8,128)(2,1)} %bitcast.30, ...), custom_call_target="tpu_custom_call" | custom-call | tf_op jit(solution)/shard_map/layer/pallas_call | solution.py:471
  218.9 0.0 copy-start.1
  218.9 3.9 %copy.24 = bf16[1,3584,256]{2,1,0:T(8,128)(2,1)} copy(bf16[1,3584,256]{1,2,0:T(8,128)(2,1)} %bitcast.28) | data formatting | bytes 3670016
  222.8 0.0 copy-done.1
  222.8 0.0 copy-start.2
  222.8 2.2 copy.25
  225.1 0.0 copy-start
  225.1 2.3 copy.29
  227.4 0.0 copy-done.2
  227.4 0.9 copy.30
  228.3 0.0 copy-done
  228.3 1.2 copy.31
  (5 shorter events, 0.1 us)
Async XLA Ops:
  218.9 3.9 %copy-start.1 = (bf16[256,3584]{1,0:T(8,128)(2,1)S(1)}, bf16[256,3584]{1,0:T(8,128)(2,1)}, u32[]{:S(2)}) copy-start(bf16[256,3584]{1,0:T(8,128)(2,1)} %get-tuple-element.13) | copy-start | bytes 5505028
  222.8 4.6 %copy-start.2 = (bf16[128,3584]{1,0:T(8,128)(2,1)S(1)}, bf16[128,3584]{1,0:T(8,128)(2,1)}, u32[]{:S(2)}) copy-start(bf16[128,3584]{1,0:T(8,128)(2,1)} %get-tuple-element.11) | copy-start | bytes 2752516
  225.1 3.2 %copy-start = (bf16[256,3584]{1,0:T(8,128)(2,1)S(1)}, bf16[256,3584]{1,0:T(8,128)(2,1)}, u32[]{:S(2)}) copy-start(bf16[256,3584]{1,0:T(8,128)(2,1)} %get-tuple-element.14) | copy-start | bytes 5505028

commit v4 on v3

--- a/solution.py
+++ b/solution.py
@@ -47,11 +47,15 @@
     grad_up,
     grad_down,
     mirror_in,
+    other_down,
     relay_weight,
+    mirror_weight,
     mine,
     raw,
+    mirror_raw,
     other,
     slots,
+    mirror_slots,
     rows,
     gate,
     up,
@@ -65,7 +69,6 @@
     out,
     halves,
     landing,
-    other_down,
     stage,
     far_send,
     far_recv,
@@ -85,10 +88,14 @@
     across_recv,
     swap_send,
     swap_recv,
-    away_sem,
+    away_send,
+    away_recv,
+    relay_send,
+    relay_recv,
     load_sem,
     stage_sem,
     result_sem,
+    free_sem,
 ):
     pipe, own, y, z, core = place()
     sibling = own + 1 - 2 * core
@@ -106,7 +113,8 @@
     barrier = pltpu.get_barrier_semaphore()
     for peer in peers[1:] + [sibling, opposite]:
         pl.semaphore_signal(barrier, inc=1, device_id=(pipe, peer), device_id_type=MESH)
-    pl.semaphore_signal(barrier, inc=1, device_id=(mirrored, own), device_id_type=MESH)
+    for peer in (own, opposite):
+        pl.semaphore_signal(barrier, inc=1, device_id=(mirrored, peer), device_id_type=MESH)
 
     loads = [
         pltpu.make_async_copy(source, target, load_sem.at[i])
@@ -118,6 +126,9 @@
                 (w_up, up),
                 (w_down, down),
                 (mirror_in, rows.at[1]),
+                (other_down, down.at[pl.ds(0, half)]),
+                (mirror_slots.at[z], mirror_in.at[own]),
+                (mirror_slots.at[4 + z], mirror_in.at[opposite]),
             )
         )
     ]
@@ -137,7 +148,22 @@
             device_id_type=MESH,
         )
 
-    away = remote(away_weight, relay_weight, away_sem.at[0], away_sem.at[1], (pipe, opposite))
+    placings = [
+        remote(source, target, away_send.at[i], away_recv.at[i], device)
+        for i, (source, target, device) in enumerate(
+            (
+                (away_weight, relay_weight, (pipe, opposite)),
+                (own_weight.at[2], mirror_weight.at[0], (mirrored, own)),
+                (away_weight.at[2], mirror_weight.at[1], (mirrored, opposite)),
+            )
+        )
+    ]
+    swap_raw = remote(
+        mine.at[0], mirror_raw.at[1], relay_send.at[1], relay_recv.at[1], (mirrored, opposite)
+    )
+    relay_raw = remote(
+        mirror_raw.at[1], mirror_raw.at[0], relay_send.at[0], relay_recv.at[0], (pipe, opposite)
+    )
 
     def cross_raw(a):
         return remote(mine.at[a], raw.at[a], raw_send.at[a], raw_recv.at[a], (pipe, opposite))
@@ -153,14 +179,16 @@
         source = target if k % 4 else slots.at[a * 8 + (k // 4) * 4 + z]
         return remote(source, target, near_send.at[a, k], near_recv.at[a, k], (pipe, sibling))
 
-    def to_mirror(k):
-        source = rows.at[0, origin(k)]
+    def mirror_far(k):
+        dz = k % 4
+        source = mirror_slots.at[(k // 4) * 4 + (z + dz) % 4]
+        target = mirror_in.at[(((y + k // 4) % 2) * 4 + z) * 2 + core]
+        return remote(source, target, mirror_send.at[k], mirror_recv.at[k], (pipe, peers[dz]))
+
+    def mirror_near(k):
         target = mirror_in.at[origin(k)]
-        return remote(source, target, mirror_send.at[k], mirror_recv.at[k], (mirrored, own))
-
-    def pass_on(k):
-        block = mirror_in.at[origin(k)]
-        return remote(block, block, pass_send.at[k], pass_recv.at[k], (pipe, sibling))
+        source = target if k % 4 else mirror_slots.at[(k // 4) * 4 + z]
+        return remote(source, target, pass_send.at[k], pass_recv.at[k], (pipe, sibling))
 
     def swap(i):
         source = down.at[pl.ds(0, half)] if i == 2 else factors.at[i, 1 - kept]
@@ -171,7 +199,7 @@
 
     def give_half(a, k):
         source = parts[a].at[chip_at(y, z, k, 1) * 2 + 1 - core]
-        target = halves.at[a, k]
+        target = halves.at[k]
         return remote(source, target, half_send.at[a, k], half_recv.at[a, k], (pipe, sibling))
 
     def along(a, k):
@@ -229,18 +257,29 @@
             far(a, 4 * side + k).wait_recv()
             near(a, 4 * side + k).start()
 
-    def mirror(side):
-        for k in range(4):
-            to_mirror(4 * side + k).start()
+    def mirror_pack(side):
+        def tile(columns):
+            total = dot(mirror_weight[side], mirror_raw[side, :, columns], (0, 0))
+            mirror_slots[side * 4 : side * 4 + 4, :, columns] = total.astype(jnp.bfloat16).reshape(
+                4, CAP, step
+            )
+
+        tiles(tile)
+
+    def mirror_send_on(side):
+        for k in (2, 1, 3):
+            mirror_far(4 * side + k).start()
+        mirror_near(4 * side).start()
+        loads[7 + side].start()
 
     def settle(a):
         for k in range(CHIPS):
             near(a, k).wait_recv()
 
-    def pass_side(side):
-        for k in range(4):
-            to_mirror(4 * side + k).wait_recv()
-            pass_on(4 * side + k).start()
+    def mirror_receive(side):
+        for k in (1, 3, 2):
+            mirror_far(4 * side + k).wait_recv()
+            mirror_near(4 * side + k).start()
 
     order = [4 * dy + dz for dy in (1, 0) for dz in (2, 1, 3, 0)]
 
@@ -248,7 +287,7 @@
         for k in order:
             here = chip_at(y, z, k, 1) * 2 + core
             give_half(a, k).wait_recv()
-            total = halves[a, k].astype(jnp.float32) + parts[a][here].astype(jnp.float32)
+            total = halves[k].astype(jnp.float32) + parts[a][here].astype(jnp.float32)
             if k % 4:
                 parts[a][here] = total.astype(jnp.bfloat16)
                 along(a, k).start()
@@ -270,9 +309,11 @@
         tiles(tile)
 
     loads[0].wait()
-    pl.semaphore_wait(barrier, 6)
-    away.start()
+    pl.semaphore_wait(barrier, 7)
+    for placing in placings:
+        placing.start()
     cross_raw(0).start()
+    swap_raw.start()
     pack(0, 0)
     send(0, 0)
     loads[1].wait()
@@ -280,17 +321,20 @@
     send(1, 0)
     cross_raw(0).wait_send()
     cross_raw(1).start()
-    away.wait()
+    placings[0].wait_recv()
     cross_raw(0).wait_recv()
     pack(0, 1)
     send(0, 1)
     receive(0, 0)
+    for placing in placings[1:]:
+        placing.wait_recv()
+    swap_raw.wait_recv()
+    mirror_pack(1)
     cross_raw(1).wait_recv()
+    relay_raw.start()
     pack(1, 1)
     send(1, 1)
-    mirror(0)
     receive(0, 1)
-    mirror(1)
     settle(0)
     for load in loads[2:5]:
         load.wait()
@@ -321,6 +365,7 @@
     tiles(out_tile)
     for k in order:
         give_half(0, k).start()
+    mirror_send_on(1)
     receive(1, 0)
     receive(1, 1)
     settle(1)
@@ -346,6 +391,7 @@
     for i in range(2):
         swap(i).start()
     add_halves(0)
+    pl.semaphore_signal(free_sem, inc=1, device_id=(pipe, sibling), device_id_type=MESH)
 
     for a in range(2):
         for k in range(CHIPS):
@@ -363,6 +409,7 @@
             )
 
     tiles(input_tile)
+    pl.semaphore_wait(free_sem, 1)
     for k in order:
         give_half(1, k).start()
 
@@ -374,12 +421,15 @@
     tiles(down_tile)
     swap(2).start()
     add_halves(1)
-    pass_side(0)
-    pass_side(1)
+    relay_raw.wait_recv()
+    mirror_pack(0)
+    mirror_send_on(0)
+    mirror_receive(1)
 
     for a in range(2):
         if a == 0:
             cross_raw(1).wait_send()
+            swap_raw.wait_send()
 
         def send_on(columns, total, a=a):
             mine[a, :, columns] = total.astype(jnp.bfloat16)
@@ -387,8 +437,11 @@
         combine(a, 1, relay_weight, send_on)
         across(a).start()
 
+    mirror_receive(0)
     for k in range(CHIPS):
-        pass_on(k).wait_recv()
+        mirror_near(k).wait_recv()
+    loads[7].wait()
+    loads[8].wait()
     loads[5].start()
     for i in range(2):
         swap(i).wait_recv()
@@ -399,7 +452,7 @@
         columns = pl.ds(pl.multiple_of(j * step, step), step)
         slot = j % 2
         return pltpu.make_async_copy(
-            stage.at[slot, i], targets[i].at[:, columns], stage_sem.at[slot, i]
+            stage.at[slot, i], targets[i].at[columns, :], stage_sem.at[slot, i]
         )
 
     def weight_tile(j, carry):
@@ -414,37 +467,44 @@
 
             total = dot(factors[i, kept], mine_rows, (1, 0))
             total += dot(mirror_factors[i], their_rows, (1, 0))
-            stage[j % 2, i] = total.astype(jnp.bfloat16)
+            stage[j % 2, i] = total.T.astype(jnp.bfloat16)
             staged(j, i).start()
         return carry
 
     lax.fori_loop(0, 7, weight_tile, 0)
 
-    for a in range(2):
+    def finish_rows(a):
         across(a).wait_recv()
 
-        def finish(columns, total, a=a):
+        def finish(columns, total):
             total = total + other[a, :, columns].astype(jnp.float32)
             raw[a, :, columns] = total.astype(jnp.bfloat16)
 
         combine(a, 0, own_weight, finish)
         results[a].start()
-    swap(2).wait_recv()
 
     def down_sum(columns):
-        total = down[half:, columns].astype(jnp.float32) + other_down[:, columns].astype(jnp.float32)
+        total = down[half:, columns].astype(jnp.float32) + down[:half, columns].astype(jnp.float32)
         down[half:, columns] = total.astype(jnp.bfloat16)
 
+    finish_rows(0)
+    swap(2).wait()
+    loads[6].start()
+    loads[6].wait()
     tiles(down_sum)
     results[2].start()
+    finish_rows(1)
 
     for j in (5, 6):
         for i in range(2):
             staged(j, i).wait()
     for result in results:
         result.wait()
-    for i in range(3):
+    for i in range(2):
         swap(i).wait_send()
+    for placing in placings:
+        placing.wait_send()
+    relay_raw.wait_send()
     for a in range(2):
         across(a).wait_send()
         for k in range(CHIPS):
@@ -452,8 +512,9 @@
             if k % 4:
                 along(a, k).wait_send()
     for k in range(CHIPS):
-        to_mirror(k).wait_send()
-        pass_on(k).wait_send()
+        mirror_near(k).wait_send()
+        if k % 4:
+            mirror_far(k).wait_send()
 
 
 def layer(tokens, grads, own_weight, away_weight, w_gate, w_up, w_down):
@@ -467,19 +528,23 @@
     blocks = (2 * CHIPS, CAP, width)
     total = 2 * CHIPS * CAP
     ours = jax.ShapeDtypeStruct((count, width), kind)
-    weight = jax.ShapeDtypeStruct((half, width), kind)
+    weight = jax.ShapeDtypeStruct((width, half), kind)
+    down = jax.ShapeDtypeStruct((half, width), kind)
     return pl.pallas_call(
         layer_kernel,
         name="layer",
-        out_shape=(ours, ours, weight, weight, weight, jax.ShapeDtypeStruct(blocks, kind)),
+        out_shape=(ours, ours, weight, weight, down, jax.ShapeDtypeStruct(blocks, kind), down),
         in_specs=[anywhere] * 2 + [vmem] + [anywhere] * 4,
-        out_specs=(anywhere,) * 6,
+        out_specs=(anywhere,) * 7,
         scratch_shapes=[
             pltpu.VMEM(own_weight.shape, kind),
+            pltpu.VMEM((2, *own_weight.shape[1:]), kind),
+            pltpu.VMEM((2, count, width), kind),
             pltpu.VMEM((2, count, width), kind),
             pltpu.VMEM((2, count, width), kind),
             pltpu.VMEM((2, count, width), kind),
             pltpu.VMEM(blocks, kind),
+            pltpu.VMEM((CHIPS, CAP, width), kind),
             pltpu.VMEM((2, *blocks), kind),
             pltpu.VMEM(w_gate.shape, kind),
             pltpu.VMEM(w_up.shape, kind),
@@ -491,16 +556,16 @@
             pltpu.VMEM((3, 2, half, total), kind),
             pltpu.VMEM((2, half, total), kind),
             pltpu.VMEM(blocks, kind),
-            pltpu.VMEM((2, CHIPS, CAP, width), kind),
+            pltpu.VMEM((CHIPS, CAP, width), kind),
             pltpu.VMEM((2, 2, 4, CAP, width), kind),
-            pltpu.VMEM((half, width), kind),
-            pltpu.VMEM((2, 2, half, width // 7), kind),
+            pltpu.VMEM((2, 2, width // 7, half), kind),
         ]
         + [dma((2, CHIPS))] * 8
         + [dma((CHIPS,))] * 4
         + [dma((2,))] * 4
-        + [dma((3,))] * 2
-        + [dma((2,)), dma((6,)), dma((2, 2)), dma((3,))],
+        + [dma((3,))] * 4
+        + [dma((2,))] * 2
+        + [dma((9,)), dma((2, 2)), dma((3,)), pltpu.SemaphoreType.REGULAR],
         compiler_params=pltpu.CompilerParams(
             collective_id=1, has_side_effects=True, vmem_limit_bytes=62 << 20
         ),
@@ -530,7 +595,7 @@
     out_acts, grad_acts, grad_gate, grad_up, grad_down = layer(
         tokens, grads, own_weight, away_weight, gate_weight, up_weight, down_weight
     )
-    return (out_acts[None], grad_acts[None], grad_gate.T[None], grad_up.T[None], grad_down[None])
+    return (out_acts[None], grad_acts[None], grad_gate[None], grad_up[None], grad_down[None])
 
 
 def solution(mesh):

time: 230 us -> 199 us (0.87)
  Pallas kernels: 215 us -> 186 us
    pallas_call x1, Pallas kernels: 215 us -> 186 us  [layer(): pl.pallas_call(layer_kernel, name='layer', out_shape=(ours, ours, weight,...]
    unnamed x12 -> x14, local copies, waits for them, and re-layouts: 11.4 us -> 9.58 us
where the time goes in v4:
time: 199 us; the launch traced here: 198 us
  Pallas kernels  186 us (93%)
  local copies, waits for them, and re-layouts  10.8 us (5%)
    pallas_call x1, Pallas kernels, layer(): pl.pallas_call(layer_kernel, name='layer', out_shape=(ours, ours, weight,...  186 us
    unnamed x14, local copies, waits for them, and re-layouts  9.58 us

profile of v4, /device:TPU:1, one launch (start us, length us, event | category | flops | bytes accessed | tf_op | source)
XLA Modules:
  0.0 198.4 jit_solution(8662427191553727961)
XLA Ops:
  0.7 0.8 copy.17
  1.5 0.1 eq.28
  1.6 0.3 fusion
  1.9 0.1 convert_element_type.55
  2.0 0.1 copy.19
  2.1 0.9 select_reduce_fusion
  3.1 0.9 constant_dynamic-slice_fusion
  4.0 185.6 %layer.1 = (bf16[128,3584]{1,0:T(8,128)(2,1)}, bf16[128,3584]{1,0:T(8,128)(2,1)}, bf16[3584,256]{1,0:T(8,128)(2,1)}, bf16[3584,256]{1,0:T(8,128)(2,1)}, bf16[256...) custom-call(bf16[128,3584]{1,0:T(8,128)(2,1)} %bitcast.25, ...), custom_call_target="tpu_custom_call" | custom-call | tf_op jit(solution)/shard_map/layer/pallas_call | solution.py:533
  189.6 0.0 copy-start.3
  189.6 0.0 copy-start.2
  189.6 2.3 %copy.25 = bf16[1,128,3584]{2,1,0:T(8,128)(2,1)} copy(bf16[1,128,3584]{2,1,0:T(8,128)(2,1)} %bitcast.28) | data formatting | bytes 1835008
  191.9 0.0 copy-done.3
  191.9 0.9 copy.26
  192.8 0.0 copy-done.2
  192.8 0.0 copy-start.1
  192.8 1.2 copy.27
  194.1 0.9 copy-done.1
  195.0 0.0 copy-start
  195.0 1.2 copy.28
  196.2 0.9 copy-done
  197.2 1.2 copy.29
  (5 shorter events, 0.1 us)
Async XLA Ops:
  189.6 2.3 %copy-start.3 = (bf16[128,3584]{1,0:T(8,128)(2,1)S(1)}, bf16[128,3584]{1,0:T(8,128)(2,1)}, u32[]{:S(2)}) copy-start(bf16[128,3584]{1,0:T(8,128)(2,1)} %get-tuple-element.11) | copy-start | bytes 2752516
  189.6 3.2 %copy-start.2 = (bf16[3584,256]{1,0:T(8,128)(2,1)S(1)}, bf16[3584,256]{1,0:T(8,128)(2,1)}, u32[]{:S(2)}) copy-start(bf16[3584,256]{1,0:T(8,128)(2,1)} %get-tuple-element.12) | copy-start | bytes 5505028
  192.8 2.2 %copy-start.1 = (bf16[3584,256]{1,0:T(8,128)(2,1)S(1)}, bf16[3584,256]{1,0:T(8,128)(2,1)}, u32[]{:S(2)}) copy-start(bf16[3584,256]{1,0:T(8,128)(2,1)} %get-tuple-element.13) | copy-start | bytes 5505028
  195.0 2.2 %copy-start = (bf16[256,3584]{1,0:T(8,128)(2,1)S(1)}, bf16[256,3584]{1,0:T(8,128)(2,1)}, u32[]{:S(2)}) copy-start(bf16[256,3584]{1,0:T(8,128)(2,1)} %get-tuple-element.14) | copy-start | bytes 5505028

commit v5 on v4

--- a/solution.py
+++ b/solution.py
@@ -22,12 +22,6 @@
     return ((y + k // 4) % 2) * 4 + (z + 4 + sign * (k % 4)) % 4
 
 
-def split_gain(gain):
-    high = lax.reduce_precision(gain, exponent_bits=8, mantissa_bits=7)
-    low = lax.reduce_precision(gain - high, exponent_bits=8, mantissa_bits=7)
-    return high.astype(jnp.bfloat16), low.astype(jnp.bfloat16)
-
-
 def dot(a, b, contract):
     dims = ((contract[:1], contract[1:]), ((), ()))
     return lax.dot_general(a, b, dims, preferred_element_type=jnp.float32)
@@ -36,24 +30,27 @@
 def layer_kernel(
     tokens,
     grads,
-    own_weight,
-    away_weight,
+    ids,
+    gain,
     w_gate,
     w_up,
     w_down,
-    out_acts,
-    grad_acts,
+    out_terms,
+    input_terms,
+    out_other,
+    input_other,
     grad_gate,
     grad_up,
-    grad_down,
+    own_down,
+    other_down,
     mirror_in,
-    other_down,
+    own_weight,
+    away_weight,
     relay_weight,
     mirror_weight,
     mine,
     raw,
     mirror_raw,
-    other,
     slots,
     mirror_slots,
     rows,
@@ -69,6 +66,7 @@
     out,
     halves,
     landing,
+    away_half,
     stage,
     far_send,
     far_recv,
@@ -88,6 +86,7 @@
     across_recv,
     swap_send,
     swap_recv,
+    down_sem,
     away_send,
     away_recv,
     relay_send,
@@ -126,7 +125,6 @@
                 (w_up, up),
                 (w_down, down),
                 (mirror_in, rows.at[1]),
-                (other_down, down.at[pl.ds(0, half)]),
                 (mirror_slots.at[z], mirror_in.at[own]),
                 (mirror_slots.at[4 + z], mirror_in.at[opposite]),
             )
@@ -190,10 +188,14 @@
         source = target if k % 4 else mirror_slots.at[(k // 4) * 4 + z]
         return remote(source, target, pass_send.at[k], pass_recv.at[k], (pipe, sibling))
 
-    def swap(i):
-        source = down.at[pl.ds(0, half)] if i == 2 else factors.at[i, 1 - kept]
-        target = other_down if i == 2 else mirror_factors.at[i]
-        return remote(source, target, swap_send.at[i], swap_recv.at[i], (mirrored, own))
+    def swap(i, side):
+        if i == 2:
+            source, target = away_half, other_down
+            return remote(source, target, down_sem.at[0], down_sem.at[1], (mirrored, own))
+        some = pl.ds(pl.multiple_of(side * group, group), group)
+        source = factors.at[i, 1 - kept, :, some]
+        target = mirror_factors.at[i, :, some]
+        return remote(source, target, swap_send.at[i, side], swap_recv.at[i, side], (mirrored, own))
 
     parts = (out, slots)
 
@@ -209,17 +211,16 @@
         return remote(source, target, along_send.at[a, k], along_recv.at[a, k], device)
 
     def across(a):
-        return remote(
-            mine.at[a], other.at[a], across_send.at[a], across_recv.at[a], (pipe, opposite)
-        )
+        target = (out_other, input_other)[a]
+        return remote(mine.at[a], target, across_send.at[a], across_recv.at[a], (pipe, opposite))
 
     results = [
         pltpu.make_async_copy(source, target, result_sem.at[i])
         for i, (source, target) in enumerate(
             (
-                (raw.at[0], out_acts),
-                (raw.at[1], grad_acts),
-                (down.at[pl.ds(half, half)], grad_down),
+                (raw.at[0], out_terms),
+                (raw.at[1], input_terms),
+                (down.at[pl.ds(half, half)], own_down),
             )
         )
     ]
@@ -239,9 +240,9 @@
         def tile(columns):
             part = source[a, :, columns]
             if a == 0:
-                total = dot(weight[2], part, (0, 0))
+                total = dot(weight[2], part, (1, 0))
             else:
-                total = dot(weight[0], part, (0, 0)) + dot(weight[1], part, (0, 0))
+                total = dot(weight[0], part, (1, 0)) + dot(weight[1], part, (1, 0))
             slots[first : first + 4, :, columns] = total.astype(jnp.bfloat16).reshape(4, CAP, step)
 
         tiles(tile)
@@ -259,7 +260,7 @@
 
     def mirror_pack(side):
         def tile(columns):
-            total = dot(mirror_weight[side], mirror_raw[side, :, columns], (0, 0))
+            total = dot(mirror_weight[side], mirror_raw[side, :, columns], (1, 0))
             mirror_slots[side * 4 : side * 4 + 4, :, columns] = total.astype(jnp.bfloat16).reshape(
                 4, CAP, step
             )
@@ -270,10 +271,10 @@
         for k in (2, 1, 3):
             mirror_far(4 * side + k).start()
         mirror_near(4 * side).start()
-        loads[7 + side].start()
-
-    def settle(a):
-        for k in range(CHIPS):
+        loads[6 + side].start()
+
+    def settle(a, ks):
+        for k in ks:
             near(a, k).wait_recv()
 
     def mirror_receive(side):
@@ -281,18 +282,22 @@
             mirror_far(4 * side + k).wait_recv()
             mirror_near(4 * side + k).start()
 
-    order = [4 * dy + dz for dy in (1, 0) for dz in (2, 1, 3, 0)]
-
-    def add_halves(a):
-        for k in order:
+    def give_halves(a):
+        for side in (1, 0):
+            for dz in (2, 1, 3, 0):
+                give_half(a, 4 * side + dz).start()
+
+    def add_halves(a, side):
+        for dz in (2, 1, 3, 0):
+            k = 4 * side + dz
             here = chip_at(y, z, k, 1) * 2 + core
             give_half(a, k).wait_recv()
             total = halves[k].astype(jnp.float32) + parts[a][here].astype(jnp.float32)
-            if k % 4:
-                parts[a][here] = total.astype(jnp.bfloat16)
-                along(a, k).start()
-            else:
-                landing[a, k // 4, z] = total.astype(jnp.bfloat16)
+            if dz == 0:
+                landing[a, side, z] = total.astype(jnp.bfloat16)
+                continue
+            parts[a][here] = total.astype(jnp.bfloat16)
+            along(a, k).start()
 
     def combine(a, dy, weight, put):
         for k in range(4 * dy + 1, 4 * dy + 4):
@@ -301,18 +306,40 @@
         def tile(columns):
             block = landing[a, dy, :, :, columns].reshape(4 * CAP, step)
             if a == 0:
-                total = dot(weight[0], block, (1, 0)) + dot(weight[1], block, (1, 0))
+                total = dot(weight[0], block, (0, 0)) + dot(weight[1], block, (0, 0))
             else:
-                total = dot(weight[2], block, (1, 0))
+                total = dot(weight[2], block, (0, 0))
             put(columns, total)
 
         tiles(tile)
+
+    count = tokens.shape[0]
+    experts = lax.broadcasted_iota(jnp.int32, (CHIPS, count), 0)
+    member = [ids[c : c + 1, :] == experts for c in range(2)]
+    chosen = jnp.where(member[0] | member[1], 1.0, 0.0).astype(jnp.bfloat16)
+    earlier = lax.broadcasted_iota(jnp.int32, (count, count), 0) < lax.broadcasted_iota(
+        jnp.int32, (count, count), 1
+    )
+    ranks_before = dot(chosen, jnp.where(earlier, 1.0, 0.0).astype(jnp.bfloat16), (1, 0))
+    slot_of = [
+        ids[c : c + 1, :] * CAP
+        + jnp.sum(jnp.where(member[c], ranks_before, 0.0), axis=0, keepdims=True).astype(jnp.int32)
+        for c in range(2)
+    ]
+    position = lax.broadcasted_iota(jnp.int32, (4 * CAP, count), 0)
+    for weight, side in ((own_weight, y), (away_weight, 1 - y)):
+        hits = [position + side * (4 * CAP) == slot_of[c] for c in range(2)]
+        value = jnp.where(hits[0], gain[0:1, :], 0.0) + jnp.where(hits[1], gain[1:2, :], 0.0)
+        high = value.astype(jnp.bfloat16)
+        weight[0] = high
+        weight[1] = (value - high.astype(jnp.float32)).astype(jnp.bfloat16)
+        weight[2] = jnp.where(hits[0] | hits[1], 1.0, 0.0).astype(jnp.bfloat16)
 
     loads[0].wait()
     pl.semaphore_wait(barrier, 7)
+    cross_raw(0).start()
     for placing in placings:
         placing.start()
-    cross_raw(0).start()
     swap_raw.start()
     pack(0, 0)
     send(0, 0)
@@ -335,7 +362,8 @@
     pack(1, 1)
     send(1, 1)
     receive(0, 1)
-    settle(0)
+    receive(1, 0)
+    settle(0, range(CHIPS))
     for load in loads[2:5]:
         load.wait()
 
@@ -355,22 +383,7 @@
 
     lax.fori_loop(0, 2, units_of, 0)
 
-    def out_tile(columns):
-        for i in range(2):
-            part = dot(hidden[i * group : i * group + group, :], down[:, columns], (1, 0))
-            out[i * CHIPS : i * CHIPS + CHIPS, :, columns] = part.astype(jnp.bfloat16).reshape(
-                CHIPS, CAP, step
-            )
-
-    tiles(out_tile)
-    for k in order:
-        give_half(0, k).start()
-    mirror_send_on(1)
-    receive(1, 0)
-    receive(1, 1)
-    settle(1)
-
-    def grads_of(i, carry):
+    def grads_of(i):
         block = rows[1, pl.ds(i * CHIPS, CHIPS)].reshape(group, width)
         here = pl.ds(pl.multiple_of(i * group, group), group)
         for j in range(2):
@@ -385,13 +398,36 @@
             up_grad[here, some] = for_up.astype(jnp.bfloat16)
             factors[0, j, :, here] = for_gate.T.astype(jnp.bfloat16)
             factors[1, j, :, here] = for_up.T.astype(jnp.bfloat16)
-        return carry
-
-    lax.fori_loop(0, 2, grads_of, 0)
+
+    settle(1, range(4))
+    grads_of(y)
+    receive(1, 1)
+    settle(1, range(4, CHIPS))
+    mirror_send_on(1)
+    grads_of(1 - y)
+    relay_raw.wait_recv()
     for i in range(2):
-        swap(i).start()
-    add_halves(0)
-    pl.semaphore_signal(free_sem, inc=1, device_id=(pipe, sibling), device_id_type=MESH)
+        for side in range(2):
+            swap(i, side).start()
+    mirror_pack(0)
+    mirror_send_on(0)
+
+    def away_down(columns):
+        block = rows[1, :, :, columns].reshape(2 * group, step)
+        away_half[:, columns] = dot(factors[2, 1 - kept], block, (1, 0)).astype(jnp.bfloat16)
+
+    tiles(away_down)
+    swap(2, 0).start()
+
+    def out_tile(columns):
+        for i in range(2):
+            part = dot(hidden[i * group : i * group + group, :], down[:, columns], (1, 0))
+            out[i * CHIPS : i * CHIPS + CHIPS, :, columns] = part.astype(jnp.bfloat16).reshape(
+                CHIPS, CAP, step
+            )
+
+    tiles(out_tile)
+    give_halves(0)
 
     for a in range(2):
         for k in range(CHIPS):
@@ -408,22 +444,21 @@
                 CHIPS, CAP, step
             )
 
+    add_halves(0, 1)
     tiles(input_tile)
+    add_halves(0, 0)
+    pl.semaphore_signal(free_sem, inc=1, device_id=(pipe, sibling), device_id_type=MESH)
     pl.semaphore_wait(free_sem, 1)
-    for k in order:
-        give_half(1, k).start()
-
-    def down_tile(columns):
+    give_halves(1)
+    add_halves(1, 1)
+    add_halves(1, 0)
+
+    def own_tile(columns):
         block = rows[1, :, :, columns].reshape(2 * group, step)
-        down[:half, columns] = dot(factors[2, 1 - kept], block, (1, 0)).astype(jnp.bfloat16)
         down[half:, columns] = dot(factors[2, kept], block, (1, 0)).astype(jnp.bfloat16)
 
-    tiles(down_tile)
-    swap(2).start()
-    add_halves(1)
-    relay_raw.wait_recv()
-    mirror_pack(0)
-    mirror_send_on(0)
+    tiles(own_tile)
+    results[2].start()
     mirror_receive(1)
 
     for a in range(2):
@@ -440,11 +475,12 @@
     mirror_receive(0)
     for k in range(CHIPS):
         mirror_near(k).wait_recv()
+    loads[6].wait()
     loads[7].wait()
-    loads[8].wait()
     loads[5].start()
     for i in range(2):
-        swap(i).wait_recv()
+        for side in range(2):
+            swap(i, side).wait_recv()
     loads[5].wait()
     targets = (grad_gate, grad_up)
 
@@ -473,27 +509,14 @@
 
     lax.fori_loop(0, 7, weight_tile, 0)
 
-    def finish_rows(a):
-        across(a).wait_recv()
-
-        def finish(columns, total):
-            total = total + other[a, :, columns].astype(jnp.float32)
+    for a in range(2):
+
+        def keep(columns, total, a=a):
             raw[a, :, columns] = total.astype(jnp.bfloat16)
 
-        combine(a, 0, own_weight, finish)
+        combine(a, 0, own_weight, keep)
         results[a].start()
-
-    def down_sum(columns):
-        total = down[half:, columns].astype(jnp.float32) + down[:half, columns].astype(jnp.float32)
-        down[half:, columns] = total.astype(jnp.bfloat16)
-
-    finish_rows(0)
-    swap(2).wait()
-    loads[6].start()
-    loads[6].wait()
-    tiles(down_sum)
-    results[2].start()
-    finish_rows(1)
+    swap(2, 0).wait()
 
     for j in (5, 6):
         for i in range(2):
@@ -501,12 +524,13 @@
     for result in results:
         result.wait()
     for i in range(2):
-        swap(i).wait_send()
+        for side in range(2):
+            swap(i, side).wait_send()
     for placing in placings:
         placing.wait_send()
     relay_raw.wait_send()
     for a in range(2):
-        across(a).wait_send()
+        across(a).wait()
         for k in range(CHIPS):
             give_half(a, k).wait_send()
             if k % 4:
@@ -517,7 +541,7 @@
             mirror_far(k).wait_send()
 
 
-def layer(tokens, grads, own_weight, away_weight, w_gate, w_up, w_down):
+def layer(tokens, grads, ids, gain, w_gate, w_up, w_down):
     count, width = tokens.shape
     units = w_gate.shape[1]
     half = units // 2
@@ -528,18 +552,20 @@
     blocks = (2 * CHIPS, CAP, width)
     total = 2 * CHIPS * CAP
     ours = jax.ShapeDtypeStruct((count, width), kind)
+    routing = pltpu.VMEM((3, total // 4, count), kind)
     weight = jax.ShapeDtypeStruct((width, half), kind)
     down = jax.ShapeDtypeStruct((half, width), kind)
     return pl.pallas_call(
         layer_kernel,
         name="layer",
-        out_shape=(ours, ours, weight, weight, down, jax.ShapeDtypeStruct(blocks, kind), down),
-        in_specs=[anywhere] * 2 + [vmem] + [anywhere] * 4,
-        out_specs=(anywhere,) * 7,
+        out_shape=(ours, ours, ours, ours, weight, weight, down, down, jax.ShapeDtypeStruct(blocks, kind)),
+        in_specs=[anywhere] * 2 + [vmem] * 2 + [anywhere] * 3,
+        out_specs=(anywhere,) * 9,
         scratch_shapes=[
-            pltpu.VMEM(own_weight.shape, kind),
-            pltpu.VMEM((2, *own_weight.shape[1:]), kind),
-            pltpu.VMEM((2, count, width), kind),
+            routing,
+            routing,
+            routing,
+            pltpu.VMEM((2, total // 4, count), kind),
             pltpu.VMEM((2, count, width), kind),
             pltpu.VMEM((2, count, width), kind),
             pltpu.VMEM((2, count, width), kind),
@@ -558,44 +584,40 @@
             pltpu.VMEM(blocks, kind),
             pltpu.VMEM((CHIPS, CAP, width), kind),
             pltpu.VMEM((2, 2, 4, CAP, width), kind),
+            pltpu.VMEM((half, width), kind),
             pltpu.VMEM((2, 2, width // 7, half), kind),
         ]
         + [dma((2, CHIPS))] * 8
         + [dma((CHIPS,))] * 4
         + [dma((2,))] * 4
-        + [dma((3,))] * 4
+        + [dma((2, 2))] * 2
+        + [dma((2,))]
+        + [dma((3,))] * 2
         + [dma((2,))] * 2
-        + [dma((9,)), dma((2, 2)), dma((3,)), pltpu.SemaphoreType.REGULAR],
+        + [dma((8,)), dma((2, 2)), dma((3,)), pltpu.SemaphoreType.REGULAR],
         compiler_params=pltpu.CompilerParams(
             collective_id=1, has_side_effects=True, vmem_limit_bytes=62 << 20
         ),
-    )(tokens, grads, own_weight, away_weight, w_gate, w_up, w_down)[:5]
+    )(tokens, grads, ids, gain, w_gate, w_up, w_down)[:8]
 
 
 def on_device(acts, grad_out, expert_ids, route_weights, w_gate, w_up, w_down):
     tokens, grads, ids, gain = acts[0], grad_out[0], expert_ids[0], route_weights[0]
     gate_weight, up_weight, down_weight = w_gate[0], w_up[0], w_down[0]
-    count, top = ids.shape
-    width = tokens.shape[1]
-    units = gate_weight.shape[1]
-
-    flat = ids.reshape(-1)
-    member = (flat[:, None] == jnp.arange(CHIPS, dtype=jnp.int32)[None, :]).astype(jnp.bfloat16)
-    before = jnp.tril(jnp.ones((count * top, count * top), jnp.bfloat16), -1)
-    rank = jnp.sum(dot(before, member, (1, 0)) * member.astype(jnp.float32), axis=1)
-    slot = (flat * CAP + rank.astype(jnp.int32)).reshape(count, top)
-    hits = (slot[:, :, None] == jnp.arange(CHIPS * CAP, dtype=jnp.int32)).astype(jnp.float32)
-    placing = jnp.sum(hits, axis=1).astype(jnp.bfloat16)
-    high, low = split_gain(jnp.sum(hits * gain[:, :, None], axis=1))
-
-    weights = jnp.stack([high, low, placing])
-    side = lax.axis_index("expert") // CHIPS
-    own_weight = lax.dynamic_slice_in_dim(weights, side * (4 * CAP), 4 * CAP, 2)
-    away_weight = lax.dynamic_slice_in_dim(weights, (1 - side) * (4 * CAP), 4 * CAP, 2)
-    out_acts, grad_acts, grad_gate, grad_up, grad_down = layer(
-        tokens, grads, own_weight, away_weight, gate_weight, up_weight, down_weight
+    out_terms, input_terms, out_other, input_other, grad_gate, grad_up, own_down, other_down = layer(
+        tokens, grads, ids.T, gain.T, gate_weight, up_weight, down_weight
     )
-    return (out_acts[None], grad_acts[None], grad_gate[None], grad_up[None], grad_down[None])
+
+    def add(a, b):
+        return (a.astype(jnp.float32) + b.astype(jnp.float32)).astype(jnp.bfloat16)[None]
+
+    return (
+        add(out_terms, out_other),
+        add(input_terms, input_other),
+        grad_gate[None],
+        grad_up[None],
+        add(own_down, other_down),
+    )
 
 
 def solution(mesh):

time: 199 us -> 186 us (0.935)
  Pallas kernels: 186 us -> 176 us
  local copies, waits for them, and re-layouts: 10.8 us -> 3.44 us
  other arithmetic: 0.96 us -> 5.49 us
    pallas_call x1, Pallas kernels: 186 us -> 176 us  [layer(): pl.pallas_call(layer_kernel, name='layer', out_shape=(ours, ours, ours, o...]
    unnamed x14 -> x10, local copies, waits for them, and re-layouts: 9.58 us -> 3.44 us
    broadcast_in_dim x0 -> x2, other arithmetic: none -> 5.49 us  [add(): (a.astype(jnp.float32) + b.astype(jnp.float32)).astype(jnp.bfloat16)[None]]
where the time goes in v5:
time: 186 us
  Pallas kernels  176 us (95%)
  other arithmetic  5.49 us (3%)
  local copies, waits for them, and re-layouts  3.44 us (2%)
    pallas_call x1, Pallas kernels, layer(): pl.pallas_call(layer_kernel, name='layer', out_shape=(ours, ours, ours, o...  176 us
    broadcast_in_dim x2, other arithmetic, add(): (a.astype(jnp.float32) + b.astype(jnp.float32)).astype(jnp.bfloat16)[None]  5.49 us

profile of v5, /device:TPU:1, one launch (start us, length us, event | category | flops | bytes accessed | tf_op | source)
XLA Modules:
  0.0 185.6 jit_solution(620359428193901699)
XLA Ops:
  0.6 176.1 %layer.1 = (bf16[128,3584]{1,0:T(8,128)(2,1)}, bf16[128,3584]{1,0:T(8,128)(2,1)}, bf16[128,3584]{1,0:T(8,128)(2,1)}, bf16[128,3584]{1,0:T(8,128)(2,1)}, bf16[358...) custom-call(bf16[128,3584]{1,0:T(8,128)(2,1)} %bitcast.24, ...), custom_call_target="tpu_custom_call" | custom-call | tf_op jit(solution)/shard_map/layer/pallas_call | solution.py:558
  176.7 0.0 copy-start.2
  176.7 0.0 copy-start.3
  176.7 3.8 %fusion.1 = (bf16[1,128,3584]{2,1,0:T(8,128)(2,1)}, bf16[1,128,3584]{2,1,0:T(8,128)(2,1)}) fusion(bf16[128,3584]{1,0:T(8,128)(2,1)} %get-tuple-element.14, bf16[128,3584]{1,0:T(8,128)(2,1)} %get-tuple-element.13, bf16[128,3584]{1,0:T(8,128)(2,1)} %get-tuple-element.16, bf16[128,3584]{1,0:T(8,128)(2,1)} %get-tuple-element.15), kind=kLoop, calls=%fused_computation.4 | loop fusion | flops 3670016 | bytes 5505024 | tf_op jit(solution)/shard_map/broadcast_in_dim | solution.py:612
  180.5 0.0 copy-done.2
  180.5 0.0 copy-done.3
  180.5 0.0 copy-start.1
  180.5 1.7 fusion
  182.2 0.0 copy-done.1
  182.3 0.0 copy-start
  182.3 1.2 copy.14
  183.5 0.9 copy-done
  184.4 1.2 copy.15
Async XLA Ops:
  176.7 3.8 %copy-start.2 = (bf16[256,3584]{1,0:T(8,128)(2,1)S(1)}, bf16[256,3584]{1,0:T(8,128)(2,1)}, u32[]{:S(2)}) copy-start(bf16[256,3584]{1,0:T(8,128)(2,1)} %get-tuple-element.19) | copy-start | bytes 5505028
  176.7 3.8 %copy-start.3 = (bf16[256,3584]{1,0:T(8,128)(2,1)S(1)}, bf16[256,3584]{1,0:T(8,128)(2,1)}, u32[]{:S(2)}) copy-start(bf16[256,3584]{1,0:T(8,128)(2,1)} %get-tuple-element.20) | copy-start | bytes 5505028
  180.5 1.7 copy-start.1
  182.3 2.2 %copy-start = (bf16[3584,256]{1,0:T(8,128)(2,1)S(1)}, bf16[3584,256]{1,0:T(8,128)(2,1)}, u32[]{:S(2)}) copy-start(bf16[3584,256]{1,0:T(8,128)(2,1)} %get-tuple-element.18) | copy-start | bytes 5505028

commit v6 on v5

--- a/solution.py
+++ b/solution.py
@@ -192,9 +192,8 @@
         if i == 2:
             source, target = away_half, other_down
             return remote(source, target, down_sem.at[0], down_sem.at[1], (mirrored, own))
-        some = pl.ds(pl.multiple_of(side * group, group), group)
-        source = factors.at[i, 1 - kept, :, some]
-        target = mirror_factors.at[i, :, some]
+        source = factors.at[i, 1 - kept, side]
+        target = mirror_factors.at[i, side]
         return remote(source, target, swap_send.at[i, side], swap_recv.at[i, side], (mirrored, own))
 
     parts = (out, slots)
@@ -282,10 +281,9 @@
             mirror_far(4 * side + k).wait_recv()
             mirror_near(4 * side + k).start()
 
-    def give_halves(a):
-        for side in (1, 0):
-            for dz in (2, 1, 3, 0):
-                give_half(a, 4 * side + dz).start()
+    def give_halves(a, side):
+        for dz in (2, 1, 3, 0):
+            give_half(a, 4 * side + dz).start()
 
     def add_halves(a, side):
         for dz in (2, 1, 3, 0):
@@ -297,7 +295,12 @@
                 landing[a, side, z] = total.astype(jnp.bfloat16)
                 continue
             parts[a][here] = total.astype(jnp.bfloat16)
-            along(a, k).start()
+            if side == 1:
+                along(a, k).start()
+
+    def over_rows(factor, a, columns):
+        total = dot(factor[0], rows[a, :CHIPS, :, columns].reshape(group, step), (1, 0))
+        return total + dot(factor[1], rows[a, CHIPS:, :, columns].reshape(group, step), (1, 0))
 
     def combine(a, dy, weight, put):
         for k in range(4 * dy + 1, 4 * dy + 4):
@@ -378,7 +381,7 @@
             pre[1, here, some] = pre_up
             value = pre_gate * jax.nn.sigmoid(pre_gate) * pre_up
             hidden[here, some] = value.astype(jnp.bfloat16)
-            factors[2, j, :, here] = value.T.astype(jnp.bfloat16)
+            factors[2, j, i] = value.T.astype(jnp.bfloat16)
         return carry
 
     lax.fori_loop(0, 2, units_of, 0)
@@ -396,25 +399,25 @@
             for_up = hidden_grad * (pre_gate * sigma)
             gate_grad[here, some] = for_gate.astype(jnp.bfloat16)
             up_grad[here, some] = for_up.astype(jnp.bfloat16)
-            factors[0, j, :, here] = for_gate.T.astype(jnp.bfloat16)
-            factors[1, j, :, here] = for_up.T.astype(jnp.bfloat16)
+            factors[0, j, i] = for_gate.T.astype(jnp.bfloat16)
+            factors[1, j, i] = for_up.T.astype(jnp.bfloat16)
 
     settle(1, range(4))
     grads_of(y)
     receive(1, 1)
     settle(1, range(4, CHIPS))
+    relay_raw.wait_recv()
+    for i in range(2):
+        swap(i, y).start()
     mirror_send_on(1)
     grads_of(1 - y)
-    relay_raw.wait_recv()
     for i in range(2):
-        for side in range(2):
-            swap(i, side).start()
+        swap(i, 1 - y).start()
     mirror_pack(0)
     mirror_send_on(0)
 
     def away_down(columns):
-        block = rows[1, :, :, columns].reshape(2 * group, step)
-        away_half[:, columns] = dot(factors[2, 1 - kept], block, (1, 0)).astype(jnp.bfloat16)
+        away_half[:, columns] = over_rows(factors.at[2, 1 - kept], 1, columns).astype(jnp.bfloat16)
 
     tiles(away_down)
     swap(2, 0).start()
@@ -427,7 +430,11 @@
             )
 
     tiles(out_tile)
-    give_halves(0)
+    give_halves(0, 1)
+    give_halves(0, 0)
+
+    def free():
+        pl.semaphore_signal(free_sem, inc=1, device_id=(pipe, sibling), device_id_type=MESH)
 
     for a in range(2):
         for k in range(CHIPS):
@@ -445,17 +452,19 @@
             )
 
     add_halves(0, 1)
+    free()
     tiles(input_tile)
+    pl.semaphore_wait(free_sem, 1)
+    give_halves(1, 1)
     add_halves(0, 0)
-    pl.semaphore_signal(free_sem, inc=1, device_id=(pipe, sibling), device_id_type=MESH)
+    free()
     pl.semaphore_wait(free_sem, 1)
-    give_halves(1)
+    give_halves(1, 0)
     add_halves(1, 1)
     add_halves(1, 0)
 
     def own_tile(columns):
-        block = rows[1, :, :, columns].reshape(2 * group, step)
-        down[half:, columns] = dot(factors[2, kept], block, (1, 0)).astype(jnp.bfloat16)
+        down[half:, columns] = over_rows(factors.at[2, kept], 1, columns).astype(jnp.bfloat16)
 
     tiles(own_tile)
     results[2].start()
@@ -471,6 +480,12 @@
 
         combine(a, 1, relay_weight, send_on)
         across(a).start()
+        if a == 0:
+            for k in (5, 6, 7):
+                along(1, k).wait_send()
+            for b in range(2):
+                for k in (1, 2, 3):
+                    along(b, k).start()
 
     mirror_receive(0)
     for k in range(CHIPS):
@@ -493,16 +508,14 @@
 
     def weight_tile(j, carry):
         columns = pl.ds(pl.multiple_of(j * step, step), step)
-        mine_rows = rows[0, :, :, columns].reshape(2 * group, step)
-        their_rows = rows[1, :, :, columns].reshape(2 * group, step)
         for i in range(2):
 
             @pl.when(j >= 2)
             def _(i=i):
                 staged(j - 2, i).wait()
 
-            total = dot(factors[i, kept], mine_rows, (1, 0))
-            total += dot(mirror_factors[i], their_rows, (1, 0))
+            total = over_rows(factors.at[i, kept], 0, columns)
+            total += over_rows(mirror_factors.at[i], 1, columns)
             stage[j % 2, i] = total.T.astype(jnp.bfloat16)
             staged(j, i).start()
         return carry
@@ -533,7 +546,7 @@
         across(a).wait()
         for k in range(CHIPS):
             give_half(a, k).wait_send()
-            if k % 4:
+            if k % 4 and (a, k // 4) != (1, 1):
                 along(a, k).wait_send()
     for k in range(CHIPS):
         mirror_near(k).wait_send()
@@ -579,8 +592,8 @@
             pltpu.VMEM((total, units), kind),
             pltpu.VMEM((total, units), kind),
             pltpu.VMEM((total, units), kind),
-            pltpu.VMEM((3, 2, half, total), kind),
-            pltpu.VMEM((2, half, total), kind),
+            pltpu.VMEM((3, 2, 2, half, total // 2), kind),
+            pltpu.VMEM((2, 2, half, total // 2), kind),
             pltpu.VMEM(blocks, kind),
             pltpu.VMEM((CHIPS, CAP, width), kind),
             pltpu.VMEM((2, 2, 4, CAP, width), kind),

time: 186 us -> 184 us (0.989)
  Pallas kernels: 176 us -> 174 us
where the time goes in v6:
time: 184 us
  Pallas kernels  174 us (95%)
  other arithmetic  5.49 us (3%)
  local copies, waits for them, and re-layouts  3.44 us (2%)
    pallas_call x1, Pallas kernels, layer(): pl.pallas_call(layer_kernel, name='layer', out_shape=(ours, ours, ours, o...  174 us
    broadcast_in_dim x2, other arithmetic, add(): (a.astype(jnp.float32) + b.astype(jnp.float32)).astype(jnp.bfloat16)[None]  5.49 us

profile of v6, /device:TPU:1, one launch (start us, length us, event | category | flops | bytes accessed | tf_op | source)
XLA Modules:
  0.0 183.8 jit_solution(13834356614887362635)
XLA Ops:
  0.6 174.2 %layer.1 = (bf16[128,3584]{1,0:T(8,128)(2,1)}, bf16[128,3584]{1,0:T(8,128)(2,1)}, bf16[128,3584]{1,0:T(8,128)(2,1)}, bf16[128,3584]{1,0:T(8,128)(2,1)}, bf16[358...) custom-call(bf16[128,3584]{1,0:T(8,128)(2,1)} %bitcast.24, ...), custom_call_target="tpu_custom_call" | custom-call | tf_op jit(solution)/shard_map/layer/pallas_call | solution.py:571
  174.8 0.0 copy-start.2
  174.8 0.0 copy-start.3
  174.9 3.8 %fusion.1 = (bf16[1,128,3584]{2,1,0:T(8,128)(2,1)}, bf16[1,128,3584]{2,1,0:T(8,128)(2,1)}) fusion(bf16[128,3584]{1,0:T(8,128)(2,1)} %get-tuple-element.14, bf16[128,3584]{1,0:T(8,128)(2,1)} %get-tuple-element.13, bf16[128,3584]{1,0:T(8,128)(2,1)} %get-tuple-element.16, bf16[128,3584]{1,0:T(8,128)(2,1)} %get-tuple-element.15), kind=kLoop, calls=%fused_computation.4 | loop fusion | flops 3670016 | bytes 5505024 | tf_op jit(solution)/shard_map/broadcast_in_dim | solution.py:625
  178.7 0.0 copy-done.2
  178.7 0.0 copy-done.3
  178.7 0.0 copy-start.1
  178.7 1.7 fusion
  180.4 0.0 copy-done.1
  180.4 0.0 copy-start
  180.4 1.2 copy.14
  181.6 0.9 copy-done
  182.6 1.2 copy.15
Async XLA Ops:
  174.8 3.8 %copy-start.2 = (bf16[256,3584]{1,0:T(8,128)(2,1)S(1)}, bf16[256,3584]{1,0:T(8,128)(2,1)}, u32[]{:S(2)}) copy-start(bf16[256,3584]{1,0:T(8,128)(2,1)} %get-tuple-element.19) | copy-start | bytes 5505028
  174.8 3.8 %copy-start.3 = (bf16[256,3584]{1,0:T(8,128)(2,1)S(1)}, bf16[256,3584]{1,0:T(8,128)(2,1)}, u32[]{:S(2)}) copy-start(bf16[256,3584]{1,0:T(8,128)(2,1)} %get-tuple-element.20) | copy-start | bytes 5505028
  178.7 1.7 copy-start.1
  180.4 2.2 %copy-start = (bf16[3584,256]{1,0:T(8,128)(2,1)S(1)}, bf16[3584,256]{1,0:T(8,128)(2,1)}, u32[]{:S(2)}) copy-start(bf16[3584,256]{1,0:T(8,128)(2,1)} %get-tuple-element.18) | copy-start | bytes 5505028

commit v7 on v6

--- a/solution.py
+++ b/solution.py
@@ -130,7 +130,7 @@
             )
         )
     ]
-    for load in loads[:5]:
+    for load in loads[:2]:
         load.start()
 
     def origin(k):
@@ -349,6 +349,8 @@
     loads[1].wait()
     pack(1, 0)
     send(1, 0)
+    for load in loads[2:5]:
+        load.start()
     cross_raw(0).wait_send()
     cross_raw(1).start()
     placings[0].wait_recv()

time: 184 us -> 184 us (level)
  no operation moved by 1% of the time
where the time goes in v7:
time: 184 us
  Pallas kernels  174 us (95%)
  other arithmetic  5.49 us (3%)
  local copies, waits for them, and re-layouts  3.44 us (2%)
    pallas_call x1, Pallas kernels, layer(): pl.pallas_call(layer_kernel, name='layer', out_shape=(ours, ours, ours, o...  174 us
    broadcast_in_dim x2, other arithmetic, add(): (a.astype(jnp.float32) + b.astype(jnp.float32)).astype(jnp.bfloat16)[None]  5.49 us

profile of v7, /device:TPU:1, one launch (start us, length us, event | category | flops | bytes accessed | tf_op | source)
XLA Modules:
  0.0 183.8 jit_solution(11880283773081061916)
XLA Ops:
  0.6 174.2 %layer.1 = (bf16[128,3584]{1,0:T(8,128)(2,1)}, bf16[128,3584]{1,0:T(8,128)(2,1)}, bf16[128,3584]{1,0:T(8,128)(2,1)}, bf16[128,3584]{1,0:T(8,128)(2,1)}, bf16[358...) custom-call(bf16[128,3584]{1,0:T(8,128)(2,1)} %bitcast.24, ...), custom_call_target="tpu_custom_call" | custom-call | tf_op jit(solution)/shard_map/layer/pallas_call | solution.py:573
  174.8 0.0 copy-start.2
  174.8 0.0 copy-start.3
  174.9 3.8 %fusion.1 = (bf16[1,128,3584]{2,1,0:T(8,128)(2,1)}, bf16[1,128,3584]{2,1,0:T(8,128)(2,1)}) fusion(bf16[128,3584]{1,0:T(8,128)(2,1)} %get-tuple-element.14, bf16[128,3584]{1,0:T(8,128)(2,1)} %get-tuple-element.13, bf16[128,3584]{1,0:T(8,128)(2,1)} %get-tuple-element.16, bf16[128,3584]{1,0:T(8,128)(2,1)} %get-tuple-element.15), kind=kLoop, calls=%fused_computation.4 | loop fusion | flops 3670016 | bytes 5505024 | tf_op jit(solution)/shard_map/broadcast_in_dim | solution.py:627
  178.7 0.0 copy-done.2
  178.7 0.0 copy-done.3
  178.7 0.0 copy-start.1
  178.7 1.7 fusion
  180.4 0.0 copy-done.1
  180.4 0.0 copy-start
  180.4 1.2 copy.14
  181.6 0.9 copy-done
  182.6 1.2 copy.15
Async XLA Ops:
  174.8 3.8 %copy-start.2 = (bf16[256,3584]{1,0:T(8,128)(2,1)S(1)}, bf16[256,3584]{1,0:T(8,128)(2,1)}, u32[]{:S(2)}) copy-start(bf16[256,3584]{1,0:T(8,128)(2,1)} %get-tuple-element.19) | copy-start | bytes 5505028
  174.8 3.8 %copy-start.3 = (bf16[256,3584]{1,0:T(8,128)(2,1)S(1)}, bf16[256,3584]{1,0:T(8,128)(2,1)}, u32[]{:S(2)}) copy-start(bf16[256,3584]{1,0:T(8,128)(2,1)} %get-tuple-element.20) | copy-start | bytes 5505028
  178.7 1.7 copy-start.1
  180.4 2.2 %copy-start = (bf16[3584,256]{1,0:T(8,128)(2,1)S(1)}, bf16[3584,256]{1,0:T(8,128)(2,1)}, u32[]{:S(2)}) copy-start(bf16[3584,256]{1,0:T(8,128)(2,1)} %get-tuple-element.18) | copy-start | bytes 5505028
